TPU v7x, 128 devices: a whole 4x4x4 slice. The times are simulated.
128 devices in a mesh: ctx: 16 (over z, x), doc: 8 (over y, core).
Axes of the slice: x: 4, y: 4, z: 4, core: 2. Of those that a mesh axis runs over, the one named last changes fastest.
Arguments:
- queries: bfloat16 [16384, 2048], P(('doc', 'ctx')), parts along dimension 0, may hold values from -4 to 4
- keys: bfloat16 [16384, 2048], P(('doc', 'ctx')), parts along dimension 0, may hold values from -4 to 4
- values: bfloat16 [16384, 2048], P(('doc', 'ctx')), parts along dimension 0, may hold values from -6 to 6
- outputs: bfloat16 [16384, 2048], P(('doc', 'ctx')), parts along dimension 0, may hold values from -2 to 2
- out_grad: bfloat16 [16384, 2048], P(('doc', 'ctx')), parts along dimension 0, may hold values from -2 to 2
- log_norm: bfloat16 [16, 16384], P(None, ('doc', 'ctx')), parts along dimension 1, may hold values from -0.5 to 12, as said below
Outputs:
- query_grad: bfloat16 [16384, 2048], P(('doc', 'ctx')), parts along dimension 0
- key_grad: bfloat16 [16384, 2048], P(('doc', 'ctx')), parts along dimension 0
- value_grad: bfloat16 [16384, 2048], P(('doc', 'ctx')), parts along dimension 0
There are 8 independent parts, one for each index of `doc`. A program takes and returns all parts, laid end to end along the dimension named above; each array names one. Nothing has to cross between parts.
Inputs may be any that keep to these rules, and one draw needn't show every extreme that they name: log_norm[h, t] lies within 1 of log(t + 1) + 0.5, t counted from 0 within the document.
All inputs are finite; a program needn't handle non-finite values.
Results may differ from a plain program's by a relative error of at most 0.0062.
Values may be sent and summed in bfloat16 or wider, within the bound.
No kernel may reach another device: no remote copies, remote signals or barrier semaphores. Data moves between devices by JAX's collectives and lax.ppermute only.
A program may use at most 64 MiB of HBM per device.

v0:
```python
import jax
import jax.numpy as jnp
from jax import lax
from jax.sharding import PartitionSpec as P

HD = 128


def shifted(value, axis, steps):
    count = lax.axis_size(axis)
    first, last = (max(0, -steps), min(count, count - steps))
    return lax.ppermute(value, axis, [(source, source + steps) for source in range(first, last)])


def head_view(array):
    return array.reshape(array.shape[0], -1, HD)


def row_delta(grad_rows, out_rows):
    product = grad_rows.astype(jnp.float32) * out_rows.astype(jnp.float32)
    return jnp.sum(product.reshape(grad_rows.shape[0], -1, HD), -1).T


def score_grads(
    query, key_rows, value_rows, grad_rows, lse_rows, delta_rows, query_block, key_block
):
    rows = query.shape[0]
    scale = HD ** (-0.5)
    scores = (
        jnp.einsum(
            "qhd,khd->hqk",
            head_view(query),
            head_view(key_rows),
            preferred_element_type=jnp.float32,
        )
        * scale
    )
    offsets = jnp.arange(rows, dtype=jnp.int32)
    query_pos = query_block * rows + offsets
    key_pos = key_block * rows + offsets
    causal = key_pos[None, :] <= query_pos[:, None]
    probs = jnp.exp(
        jnp.where(causal[None], scores - lse_rows.astype(jnp.float32)[:, :, None], -1e30)
    )
    dprobs = jnp.einsum(
        "qhd,khd->hqk",
        head_view(grad_rows),
        head_view(value_rows),
        preferred_element_type=jnp.float32,
    )
    dscores = probs * (dprobs - delta_rows[:, :, None])
    return (probs.astype(jnp.bfloat16), dscores.astype(jnp.bfloat16))


def query_term(dscores_low, key_rows):
    rows = key_rows.shape[0]
    part = jnp.einsum(
        "hqk,khd->qhd", dscores_low, head_view(key_rows), preferred_element_type=jnp.float32
    )
    return part.reshape(rows, -1) * HD ** (-0.5)


def key_value_terms(probs_low, dscores_low, query, grad_rows):
    rows = query.shape[0]
    value_part = jnp.einsum(
        "hqk,qhd->khd", probs_low, head_view(grad_rows), preferred_element_type=jnp.float32
    )
    key_part = jnp.einsum(
        "hqk,qhd->khd", dscores_low, head_view(query), preferred_element_type=jnp.float32
    )
    return (key_part.reshape(rows, -1) * HD ** (-0.5), value_part.reshape(rows, -1))


def local(queries, keys, values, outputs, out_grad, log_norm):
    rows, width = queries.shape
    count = lax.axis_size("ctx")
    here = lax.axis_index("ctx")
    empty = jnp.zeros((rows, width), jnp.float32)
    delta = row_delta(out_grad, outputs)
    probs_low, dscores_low = score_grads(
        queries, keys, values, out_grad, log_norm, delta, here, here
    )
    query_acc = query_term(dscores_low, keys)
    key_acc, value_acc = key_value_terms(probs_low, dscores_low, queries, out_grad)

    def advance(step, carry):
        held_keys, travel, query_acc, key_acc, value_acc = carry
        held_keys = shifted((held_keys[0], held_keys[1]), "ctx", 1)
        travel = shifted((travel[0], travel[1], travel[2], travel[3]), "ctx", -1)
        source = here - step
        target = here + step

        def own_queries():
            probs_low, dscores_low = score_grads(
                queries, held_keys[0], held_keys[1], out_grad, log_norm, delta, here, source
            )
            return query_term(dscores_low, held_keys[0])

        def own_keys():
            far_delta = row_delta(travel[1], travel[2])
            probs_low, dscores_low = score_grads(
                travel[0], keys, values, travel[1], travel[3], far_delta, target, here
            )
            return key_value_terms(probs_low, dscores_low, travel[0], travel[1])

        query_acc = query_acc + lax.cond(source >= 0, own_queries, lambda: empty)
        key_part, value_part = lax.cond(target < count, own_keys, lambda: (empty, empty))
        return (held_keys, travel, query_acc, key_acc + key_part, value_acc + value_part)

    start = ((keys, values), (queries, out_grad, outputs, log_norm), query_acc, key_acc, value_acc)
    final = lax.fori_loop(1, count, advance, start)
    query_done, key_acc, value_acc = (final[2], final[3], final[4])
    return (
        query_done.astype(jnp.bfloat16),
        key_acc.astype(jnp.bfloat16),
        value_acc.astype(jnp.bfloat16),
    )


def solution(mesh):
    in_specs = (
        P(("doc", "ctx"), None),
        P(("doc", "ctx"), None),
        P(("doc", "ctx"), None),
        P(("doc", "ctx"), None),
        P(("doc", "ctx"), None),
        P(None, ("doc", "ctx")),
    )
    out_specs = (P(("doc", "ctx"), None), P(("doc", "ctx"), None), P(("doc", "ctx"), None))
    return jax.shard_map(local, mesh=mesh, in_specs=in_specs, out_specs=out_specs, check_vma=False)
```

profile of v0, /device:TPU:0, one launch (start us, length us, event | category | flops | bytes accessed | tf_op | source)
XLA Modules:
  0.0 889.5 jit_solution(2307214393075278360)
XLA Ops:
  20.6 864.1 %while.29 = (s32[]{:T(128)}, bf16[128,2048]{0,1:T(8,128)(2,1)S(1)}, bf16[128,2048]{1,0:T(8,128)(2,1)}, bf16[128,2048]{0,1:T(8,128)(2,1)}, bf16[128,2048]{0,1:T(8...) while((s32[]{:T(128)}, bf16[128,2048]{0,1:T(8,128)(2,1)S(1)}, ...), condition=%wide.region_7.8_spmd, body=%wide.region_1.7_spmd.sunk | while | flops 475564544 | bytes 63599500 | solution.py:111
  39.1 9.5 %collective-permute-done = bf16[128,2048]{0,1:T(8,128)(2,1)} collective-permute-done((bf16[128,2048]{0,1:T(8,128)(2,1)S(1)}, bf16[128,2048]{0,1:T(8,128)(2,1)}, u32[]{:S(2)}, u32[]{:S(2)}) %collective-permute-start) | collective-permute-done | bytes 524320 | tf_op jit(solution)/shard_map/while/body/eval_jaxpr/ppermute | solution.py:12
  51.0 7.9 collective-permute-done.3
  58.9 9.3 %collective-permute-done.2 = bf16[128,2048]{0,1:T(8,128)(2,1)} collective-permute-done((bf16[128,2048]{0,1:T(8,128)(2,1)}, bf16[128,2048]{0,1:T(8,128)(2,1)}, u32[]{:S(2)}, u32[]{:S(2)}) %collective-permute-start.2) | collective-permute-done | bytes 524320 | tf_op jit(solution)/shard_map/while/body/eval_jaxpr/ppermute | solution.py:12
  68.2 8.0 conditional.5
  104.8 8.5 collective-permute-done
  115.6 9.4 %collective-permute-done.3 = bf16[128,2048]{0,1:T(8,128)(2,1)S(1)} collective-permute-done((bf16[128,2048]{0,1:T(8,128)(2,1)}, bf16[128,2048]{0,1:T(8,128)(2,1)S(1)}, u32[]{:S(2)}, u32[]{:S(2)}) %collective-permute-start.3) | collective-permute-done | bytes 524320 | tf_op jit(solution)/shard_map/while/body/eval_jaxpr/ppermute | solution.py:12
  125.1 7.8 collective-permute-done.2
  132.9 8.0 conditional.5
  152.0 6.3 collective-permute-start.1
  170.9 7.0 collective-permute-done
  180.3 10.9 %collective-permute-done.3 = bf16[128,2048]{0,1:T(8,128)(2,1)S(1)} collective-permute-done((bf16[128,2048]{0,1:T(8,128)(2,1)}, bf16[128,2048]{0,1:T(8,128)(2,1)S(1)}, u32[]{:S(2)}, u32[]{:S(2)}) %collective-permute-start.3) | collective-permute-done | bytes 524320 | tf_op jit(solution)/shard_map/while/body/eval_jaxpr/ppermute | solution.py:12
  191.2 6.3 collective-permute-done.2
  197.5 8.0 conditional.5
  216.6 6.3 collective-permute-start.1
  244.6 10.3 %collective-permute-done.3 = bf16[128,2048]{0,1:T(8,128)(2,1)S(1)} collective-permute-done((bf16[128,2048]{0,1:T(8,128)(2,1)}, bf16[128,2048]{0,1:T(8,128)(2,1)S(1)}, u32[]{:S(2)}, u32[]{:S(2)}) %collective-permute-start.3) | collective-permute-done | bytes 524320 | tf_op jit(solution)/shard_map/while/body/eval_jaxpr/ppermute | solution.py:12
  254.9 5.7 collective-permute-done.2
  260.6 8.0 conditional.5
  279.7 6.3 collective-permute-start.1
  307.7 8.7 collective-permute-done.3
  322.1 8.0 conditional.5
  341.2 6.3 collective-permute-start.1
  369.3 7.1 collective-permute-done.3
  376.3 5.7 collective-permute-done.2
  382.1 8.0 conditional.5
  401.1 6.3 collective-permute-start.1
  423.2 6.0 collective-permute-done.4
  434.8 5.7 collective-permute-done.2
  440.5 8.0 conditional.5
  459.5 6.2 collective-permute-start.1
  491.5 5.7 collective-permute-done.2
  497.2 8.0 conditional.5
  516.3 6.4 collective-permute-start.1
  547.0 5.7 collective-permute-done.2
  552.7 8.0 conditional.5
  571.8 6.3 collective-permute-start.1
  601.0 5.7 collective-permute-done.2
  606.7 8.0 conditional.5
  625.8 6.3 collective-permute-start.1
  659.4 8.0 conditional.5
  678.5 6.1 collective-permute-start.1
  706.2 5.7 collective-permute-done.2
  711.9 8.0 conditional.5
  731.0 6.0 collective-permute-start.1
  764.3 8.0 conditional.5
  783.4 6.0 collective-permute-start.1
  816.7 8.0 conditional.5
  866.9 8.0 conditional.5
  (682 shorter events, 663.8 us)
Async XLA Ops:
  21.9 17.2 %collective-permute-start.1 = (bf16[128,2048]{1,0:T(8,128)(2,1)}, bf16[128,2048]{1,0:T(8,128)(2,1)S(1)}, u32[]{:S(2)}, u32[]{:S(2)}) collective-permute-start(bf16[128,2048]{1,0:T(8,128)(2,1)} %get-tuple-element.580), channel_id=1, source_target_pairs={{0,8},{8,16},{16,24},{24,32},{32,40},{40,48},{48,56},{56,64},{64,7... | collective-permute-start | bytes 1572872 | tf_op jit(solution)/shard_map/while/body/eval_jaxpr/ppermute | solution.py:12
  26.5 22.1 %collective-permute-start = (bf16[128,2048]{0,1:T(8,128)(2,1)S(1)}, bf16[128,2048]{0,1:T(8,128)(2,1)}, u32[]{:S(2)}, u32[]{:S(2)}) collective-permute-start(bf16[128,2048]{0,1:T(8,128)(2,1)S(1)} %get-tuple-element.579), channel_id=1, source_target_pairs={{0,8},{8,16},{16,24},{24,32},{32,40},{40,48},{48,56},{56,64},{64,7... | collective-permute-start | bytes 1572872 | tf_op jit(solution)/shard_map/while/body/eval_jaxpr/ppermute | solution.py:12
  30.8 20.3 %collective-permute-start.4 = (bf16[128,2048]{0,1:T(8,128)(2,1)}, bf16[128,2048]{0,1:T(8,128)(2,1)}, u32[]{:S(2)}, u32[]{:S(2)}) collective-permute-start(bf16[128,2048]{0,1:T(8,128)(2,1)} %get-tuple-element.583), channel_id=1, source_target_pairs={{8,0},{16,8},{24,16},{32,24},{40,32},{48,40},{56,48},{64,56},{72,6... | collective-permute-start | bytes 1572872 | tf_op jit(solution)/shard_map/while/body/eval_jaxpr/ppermute | solution.py:12
  32.0 26.9 %collective-permute-start.3 = (bf16[128,2048]{0,1:T(8,128)(2,1)}, bf16[128,2048]{0,1:T(8,128)(2,1)S(1)}, u32[]{:S(2)}, u32[]{:S(2)}) collective-permute-start(bf16[128,2048]{0,1:T(8,128)(2,1)} %get-tuple-element.582), channel_id=1, source_target_pairs={{8,0},{16,8},{24,16},{32,24},{40,32},{48,40},{56,48},{64,56},{72,6... | collective-permute-start | bytes 1572872 | tf_op jit(solution)/shard_map/while/body/eval_jaxpr/ppermute | solution.py:12
  33.4 34.9 %collective-permute-start.2 = (bf16[128,2048]{0,1:T(8,128)(2,1)}, bf16[128,2048]{0,1:T(8,128)(2,1)}, u32[]{:S(2)}, u32[]{:S(2)}) collective-permute-start(bf16[128,2048]{0,1:T(8,128)(2,1)} %get-tuple-element.581), channel_id=1, source_target_pairs={{8,0},{16,8},{24,16},{32,24},{40,32},{48,40},{56,48},{64,56},{72,6... | collective-permute-start | bytes 1572872 | tf_op jit(solution)/shard_map/while/body/eval_jaxpr/ppermute | solution.py:12
  87.3 17.5 %collective-permute-start.1 = (bf16[128,2048]{1,0:T(8,128)(2,1)}, bf16[128,2048]{1,0:T(8,128)(2,1)S(1)}, u32[]{:S(2)}, u32[]{:S(2)}) collective-permute-start(bf16[128,2048]{1,0:T(8,128)(2,1)} %get-tuple-element.580), channel_id=1, source_target_pairs={{0,8},{8,16},{16,24},{24,32},{32,40},{40,48},{48,56},{56,64},{64,7... | collective-permute-start | bytes 1572872 | tf_op jit(solution)/shard_map/while/body/eval_jaxpr/ppermute | solution.py:12
  92.2 21.1 %collective-permute-start = (bf16[128,2048]{0,1:T(8,128)(2,1)S(1)}, bf16[128,2048]{0,1:T(8,128)(2,1)}, u32[]{:S(2)}, u32[]{:S(2)}) collective-permute-start(bf16[128,2048]{0,1:T(8,128)(2,1)S(1)} %get-tuple-element.579), channel_id=1, source_target_pairs={{0,8},{8,16},{16,24},{24,32},{32,40},{40,48},{48,56},{56,64},{64,7... | collective-permute-start | bytes 1572872 | tf_op jit(solution)/shard_map/while/body/eval_jaxpr/ppermute | solution.py:12
  96.9 18.8 %collective-permute-start.4 = (bf16[128,2048]{0,1:T(8,128)(2,1)}, bf16[128,2048]{0,1:T(8,128)(2,1)}, u32[]{:S(2)}, u32[]{:S(2)}) collective-permute-start(bf16[128,2048]{0,1:T(8,128)(2,1)} %get-tuple-element.583), channel_id=1, source_target_pairs={{8,0},{16,8},{24,16},{32,24},{40,32},{48,40},{56,48},{64,56},{72,6... | collective-permute-start | bytes 1572872 | tf_op jit(solution)/shard_map/while/body/eval_jaxpr/ppermute | solution.py:12
  98.2 26.9 %collective-permute-start.3 = (bf16[128,2048]{0,1:T(8,128)(2,1)}, bf16[128,2048]{0,1:T(8,128)(2,1)S(1)}, u32[]{:S(2)}, u32[]{:S(2)}) collective-permute-start(bf16[128,2048]{0,1:T(8,128)(2,1)} %get-tuple-element.582), channel_id=1, source_target_pairs={{8,0},{16,8},{24,16},{32,24},{40,32},{48,40},{56,48},{64,56},{72,6... | collective-permute-start | bytes 1572872 | tf_op jit(solution)/shard_map/while/body/eval_jaxpr/ppermute | solution.py:12
  99.5 33.4 %collective-permute-start.2 = (bf16[128,2048]{0,1:T(8,128)(2,1)}, bf16[128,2048]{0,1:T(8,128)(2,1)}, u32[]{:S(2)}, u32[]{:S(2)}) collective-permute-start(bf16[128,2048]{0,1:T(8,128)(2,1)} %get-tuple-element.581), channel_id=1, source_target_pairs={{8,0},{16,8},{24,16},{32,24},{40,32},{48,40},{56,48},{64,56},{72,6... | collective-permute-start | bytes 1572872 | tf_op jit(solution)/shard_map/while/body/eval_jaxpr/ppermute | solution.py:12
  152.0 18.9 %collective-permute-start.1 = (bf16[128,2048]{1,0:T(8,128)(2,1)}, bf16[128,2048]{1,0:T(8,128)(2,1)S(1)}, u32[]{:S(2)}, u32[]{:S(2)}) collective-permute-start(bf16[128,2048]{1,0:T(8,128)(2,1)} %get-tuple-element.580), channel_id=1, source_target_pairs={{0,8},{8,16},{16,24},{24,32},{32,40},{40,48},{48,56},{56,64},{64,7... | collective-permute-start | bytes 1572872 | tf_op jit(solution)/shard_map/while/body/eval_jaxpr/ppermute | solution.py:12
  158.3 19.6 %collective-permute-start = (bf16[128,2048]{0,1:T(8,128)(2,1)S(1)}, bf16[128,2048]{0,1:T(8,128)(2,1)}, u32[]{:S(2)}, u32[]{:S(2)}) collective-permute-start(bf16[128,2048]{0,1:T(8,128)(2,1)S(1)} %get-tuple-element.579), channel_id=1, source_target_pairs={{0,8},{8,16},{16,24},{24,32},{32,40},{40,48},{48,56},{56,64},{64,7... | collective-permute-start | bytes 1572872 | tf_op jit(solution)/shard_map/while/body/eval_jaxpr/ppermute | solution.py:12
  163.0 17.3 %collective-permute-start.4 = (bf16[128,2048]{0,1:T(8,128)(2,1)}, bf16[128,2048]{0,1:T(8,128)(2,1)}, u32[]{:S(2)}, u32[]{:S(2)}) collective-permute-start(bf16[128,2048]{0,1:T(8,128)(2,1)} %get-tuple-element.583), channel_id=1, source_target_pairs={{8,0},{16,8},{24,16},{32,24},{40,32},{48,40},{56,48},{64,56},{72,6... | collective-permute-start | bytes 1572872 | tf_op jit(solution)/shard_map/while/body/eval_jaxpr/ppermute | solution.py:12
  164.2 26.9 %collective-permute-start.3 = (bf16[128,2048]{0,1:T(8,128)(2,1)}, bf16[128,2048]{0,1:T(8,128)(2,1)S(1)}, u32[]{:S(2)}, u32[]{:S(2)}) collective-permute-start(bf16[128,2048]{0,1:T(8,128)(2,1)} %get-tuple-element.582), channel_id=1, source_target_pairs={{8,0},{16,8},{24,16},{32,24},{40,32},{48,40},{56,48},{64,56},{72,6... | collective-permute-start | bytes 1572872 | tf_op jit(solution)/shard_map/while/body/eval_jaxpr/ppermute | solution.py:12
  165.6 31.9 %collective-permute-start.2 = (bf16[128,2048]{0,1:T(8,128)(2,1)}, bf16[128,2048]{0,1:T(8,128)(2,1)}, u32[]{:S(2)}, u32[]{:S(2)}) collective-permute-start(bf16[128,2048]{0,1:T(8,128)(2,1)} %get-tuple-element.581), channel_id=1, source_target_pairs={{8,0},{16,8},{24,16},{32,24},{40,32},{48,40},{56,48},{64,56},{72,6... | collective-permute-start | bytes 1572872 | tf_op jit(solution)/shard_map/while/body/eval_jaxpr/ppermute | solution.py:12
  216.6 18.9 %collective-permute-start.1 = (bf16[128,2048]{1,0:T(8,128)(2,1)}, bf16[128,2048]{1,0:T(8,128)(2,1)S(1)}, u32[]{:S(2)}, u32[]{:S(2)}) collective-permute-start(bf16[128,2048]{1,0:T(8,128)(2,1)} %get-tuple-element.580), channel_id=1, source_target_pairs={{0,8},{8,16},{16,24},{24,32},{32,40},{40,48},{48,56},{56,64},{64,7... | collective-permute-start | bytes 1572872 | tf_op jit(solution)/shard_map/while/body/eval_jaxpr/ppermute | solution.py:12
  222.9 18.1 %collective-permute-start = (bf16[128,2048]{0,1:T(8,128)(2,1)S(1)}, bf16[128,2048]{0,1:T(8,128)(2,1)}, u32[]{:S(2)}, u32[]{:S(2)}) collective-permute-start(bf16[128,2048]{0,1:T(8,128)(2,1)S(1)} %get-tuple-element.579), channel_id=1, source_target_pairs={{0,8},{8,16},{16,24},{24,32},{32,40},{40,48},{48,56},{56,64},{64,7... | collective-permute-start | bytes 1572872 | tf_op jit(solution)/shard_map/while/body/eval_jaxpr/ppermute | solution.py:12
  227.6 17.1 %collective-permute-start.4 = (bf16[128,2048]{0,1:T(8,128)(2,1)}, bf16[128,2048]{0,1:T(8,128)(2,1)}, u32[]{:S(2)}, u32[]{:S(2)}) collective-permute-start(bf16[128,2048]{0,1:T(8,128)(2,1)} %get-tuple-element.583), channel_id=1, source_target_pairs={{8,0},{16,8},{24,16},{32,24},{40,32},{48,40},{56,48},{64,56},{72,6... | collective-permute-start | bytes 1572872 | tf_op jit(solution)/shard_map/while/body/eval_jaxpr/ppermute | solution.py:12
  228.9 26.0 %collective-permute-start.3 = (bf16[128,2048]{0,1:T(8,128)(2,1)}, bf16[128,2048]{0,1:T(8,128)(2,1)S(1)}, u32[]{:S(2)}, u32[]{:S(2)}) collective-permute-start(bf16[128,2048]{0,1:T(8,128)(2,1)} %get-tuple-element.582), channel_id=1, source_target_pairs={{8,0},{16,8},{24,16},{32,24},{40,32},{48,40},{56,48},{64,56},{72,6... | collective-permute-start | bytes 1572872 | tf_op jit(solution)/shard_map/while/body/eval_jaxpr/ppermute | solution.py:12
  230.2 30.4 %collective-permute-start.2 = (bf16[128,2048]{0,1:T(8,128)(2,1)}, bf16[128,2048]{0,1:T(8,128)(2,1)}, u32[]{:S(2)}, u32[]{:S(2)}) collective-permute-start(bf16[128,2048]{0,1:T(8,128)(2,1)} %get-tuple-element.581), channel_id=1, source_target_pairs={{8,0},{16,8},{24,16},{32,24},{40,32},{48,40},{56,48},{64,56},{72,6... | collective-permute-start | bytes 1572872 | tf_op jit(solution)/shard_map/while/body/eval_jaxpr/ppermute | solution.py:12
  279.7 17.3 %collective-permute-start.1 = (bf16[128,2048]{1,0:T(8,128)(2,1)}, bf16[128,2048]{1,0:T(8,128)(2,1)S(1)}, u32[]{:S(2)}, u32[]{:S(2)}) collective-permute-start(bf16[128,2048]{1,0:T(8,128)(2,1)} %get-tuple-element.580), channel_id=1, source_target_pairs={{0,8},{8,16},{16,24},{24,32},{32,40},{40,48},{48,56},{56,64},{64,7... | collective-permute-start | bytes 1572872 | tf_op jit(solution)/shard_map/while/body/eval_jaxpr/ppermute | solution.py:12
  286.0 16.5 %collective-permute-start = (bf16[128,2048]{0,1:T(8,128)(2,1)S(1)}, bf16[128,2048]{0,1:T(8,128)(2,1)}, u32[]{:S(2)}, u32[]{:S(2)}) collective-permute-start(bf16[128,2048]{0,1:T(8,128)(2,1)S(1)} %get-tuple-element.579), channel_id=1, source_target_pairs={{0,8},{8,16},{16,24},{24,32},{32,40},{40,48},{48,56},{56,64},{64,7... | collective-permute-start | bytes 1572872 | tf_op jit(solution)/shard_map/while/body/eval_jaxpr/ppermute | solution.py:12
  290.7 17.1 %collective-permute-start.4 = (bf16[128,2048]{0,1:T(8,128)(2,1)}, bf16[128,2048]{0,1:T(8,128)(2,1)}, u32[]{:S(2)}, u32[]{:S(2)}) collective-permute-start(bf16[128,2048]{0,1:T(8,128)(2,1)} %get-tuple-element.583), channel_id=1, source_target_pairs={{8,0},{16,8},{24,16},{32,24},{40,32},{48,40},{56,48},{64,56},{72,6... | collective-permute-start | bytes 1572872 | tf_op jit(solution)/shard_map/while/body/eval_jaxpr/ppermute | solution.py:12
  292.0 24.4 %collective-permute-start.3 = (bf16[128,2048]{0,1:T(8,128)(2,1)}, bf16[128,2048]{0,1:T(8,128)(2,1)S(1)}, u32[]{:S(2)}, u32[]{:S(2)}) collective-permute-start(bf16[128,2048]{0,1:T(8,128)(2,1)} %get-tuple-element.582), channel_id=1, source_target_pairs={{8,0},{16,8},{24,16},{32,24},{40,32},{48,40},{56,48},{64,56},{72,6... | collective-permute-start | bytes 1572872 | tf_op jit(solution)/shard_map/while/body/eval_jaxpr/ppermute | solution.py:12
  293.3 28.9 %collective-permute-start.2 = (bf16[128,2048]{0,1:T(8,128)(2,1)}, bf16[128,2048]{0,1:T(8,128)(2,1)}, u32[]{:S(2)}, u32[]{:S(2)}) collective-permute-start(bf16[128,2048]{0,1:T(8,128)(2,1)} %get-tuple-element.581), channel_id=1, source_target_pairs={{8,0},{16,8},{24,16},{32,24},{40,32},{48,40},{56,48},{64,56},{72,6... | collective-permute-start | bytes 1572872 | tf_op jit(solution)/shard_map/while/body/eval_jaxpr/ppermute | solution.py:12
  341.2 15.7 %collective-permute-start.1 = (bf16[128,2048]{1,0:T(8,128)(2,1)}, bf16[128,2048]{1,0:T(8,128)(2,1)S(1)}, u32[]{:S(2)}, u32[]{:S(2)}) collective-permute-start(bf16[128,2048]{1,0:T(8,128)(2,1)} %get-tuple-element.580), channel_id=1, source_target_pairs={{0,8},{8,16},{16,24},{24,32},{32,40},{40,48},{48,56},{56,64},{64,7... | collective-permute-start | bytes 1572872 | tf_op jit(solution)/shard_map/while/body/eval_jaxpr/ppermute | solution.py:12
  352.2 17.1 %collective-permute-start.4 = (bf16[128,2048]{0,1:T(8,128)(2,1)}, bf16[128,2048]{0,1:T(8,128)(2,1)}, u32[]{:S(2)}, u32[]{:S(2)}) collective-permute-start(bf16[128,2048]{0,1:T(8,128)(2,1)} %get-tuple-element.583), channel_id=1, source_target_pairs={{8,0},{16,8},{24,16},{32,24},{40,32},{48,40},{56,48},{64,56},{72,6... | collective-permute-start | bytes 1572872 | tf_op jit(solution)/shard_map/while/body/eval_jaxpr/ppermute | solution.py:12
  353.5 22.9 %collective-permute-start.3 = (bf16[128,2048]{0,1:T(8,128)(2,1)}, bf16[128,2048]{0,1:T(8,128)(2,1)S(1)}, u32[]{:S(2)}, u32[]{:S(2)}) collective-permute-start(bf16[128,2048]{0,1:T(8,128)(2,1)} %get-tuple-element.582), channel_id=1, source_target_pairs={{8,0},{16,8},{24,16},{32,24},{40,32},{48,40},{56,48},{64,56},{72,6... | collective-permute-start | bytes 1572872 | tf_op jit(solution)/shard_map/while/body/eval_jaxpr/ppermute | solution.py:12
  354.8 27.3 %collective-permute-start.2 = (bf16[128,2048]{0,1:T(8,128)(2,1)}, bf16[128,2048]{0,1:T(8,128)(2,1)}, u32[]{:S(2)}, u32[]{:S(2)}) collective-permute-start(bf16[128,2048]{0,1:T(8,128)(2,1)} %get-tuple-element.581), channel_id=1, source_target_pairs={{8,0},{16,8},{24,16},{32,24},{40,32},{48,40},{56,48},{64,56},{72,6... | collective-permute-start | bytes 1572872 | tf_op jit(solution)/shard_map/while/body/eval_jaxpr/ppermute | solution.py:12
  412.1 17.1 %collective-permute-start.4 = (bf16[128,2048]{0,1:T(8,128)(2,1)}, bf16[128,2048]{0,1:T(8,128)(2,1)}, u32[]{:S(2)}, u32[]{:S(2)}) collective-permute-start(bf16[128,2048]{0,1:T(8,128)(2,1)} %get-tuple-element.583), channel_id=1, source_target_pairs={{8,0},{16,8},{24,16},{32,24},{40,32},{48,40},{56,48},{64,56},{72,6... | collective-permute-start | bytes 1572872 | tf_op jit(solution)/shard_map/while/body/eval_jaxpr/ppermute | solution.py:12
  413.4 21.3 %collective-permute-start.3 = (bf16[128,2048]{0,1:T(8,128)(2,1)}, bf16[128,2048]{0,1:T(8,128)(2,1)S(1)}, u32[]{:S(2)}, u32[]{:S(2)}) collective-permute-start(bf16[128,2048]{0,1:T(8,128)(2,1)} %get-tuple-element.582), channel_id=1, source_target_pairs={{8,0},{16,8},{24,16},{32,24},{40,32},{48,40},{56,48},{64,56},{72,6... | collective-permute-start | bytes 1572872 | tf_op jit(solution)/shard_map/while/body/eval_jaxpr/ppermute | solution.py:12
  414.7 25.7 %collective-permute-start.2 = (bf16[128,2048]{0,1:T(8,128)(2,1)}, bf16[128,2048]{0,1:T(8,128)(2,1)}, u32[]{:S(2)}, u32[]{:S(2)}) collective-permute-start(bf16[128,2048]{0,1:T(8,128)(2,1)} %get-tuple-element.581), channel_id=1, source_target_pairs={{8,0},{16,8},{24,16},{32,24},{40,32},{48,40},{56,48},{64,56},{72,6... | collective-permute-start | bytes 1572872 | tf_op jit(solution)/shard_map/while/body/eval_jaxpr/ppermute | solution.py:12
  471.8 19.7 %collective-permute-start.3 = (bf16[128,2048]{0,1:T(8,128)(2,1)}, bf16[128,2048]{0,1:T(8,128)(2,1)S(1)}, u32[]{:S(2)}, u32[]{:S(2)}) collective-permute-start(bf16[128,2048]{0,1:T(8,128)(2,1)} %get-tuple-element.582), channel_id=1, source_target_pairs={{8,0},{16,8},{24,16},{32,24},{40,32},{48,40},{56,48},{64,56},{72,6... | collective-permute-start | bytes 1572872 | tf_op jit(solution)/shard_map/while/body/eval_jaxpr/ppermute | solution.py:12
  473.1 24.1 %collective-permute-start.2 = (bf16[128,2048]{0,1:T(8,128)(2,1)}, bf16[128,2048]{0,1:T(8,128)(2,1)}, u32[]{:S(2)}, u32[]{:S(2)}) collective-permute-start(bf16[128,2048]{0,1:T(8,128)(2,1)} %get-tuple-element.581), channel_id=1, source_target_pairs={{8,0},{16,8},{24,16},{32,24},{40,32},{48,40},{56,48},{64,56},{72,6... | collective-permute-start | bytes 1572872 | tf_op jit(solution)/shard_map/while/body/eval_jaxpr/ppermute | solution.py:12
  528.7 18.3 %collective-permute-start.3 = (bf16[128,2048]{0,1:T(8,128)(2,1)}, bf16[128,2048]{0,1:T(8,128)(2,1)S(1)}, u32[]{:S(2)}, u32[]{:S(2)}) collective-permute-start(bf16[128,2048]{0,1:T(8,128)(2,1)} %get-tuple-element.582), channel_id=1, source_target_pairs={{8,0},{16,8},{24,16},{32,24},{40,32},{48,40},{56,48},{64,56},{72,6... | collective-permute-start | bytes 1572872 | tf_op jit(solution)/shard_map/while/body/eval_jaxpr/ppermute | solution.py:12
  530.0 22.7 %collective-permute-start.2 = (bf16[128,2048]{0,1:T(8,128)(2,1)}, bf16[128,2048]{0,1:T(8,128)(2,1)}, u32[]{:S(2)}, u32[]{:S(2)}) collective-permute-start(bf16[128,2048]{0,1:T(8,128)(2,1)} %get-tuple-element.581), channel_id=1, source_target_pairs={{8,0},{16,8},{24,16},{32,24},{40,32},{48,40},{56,48},{64,56},{72,6... | collective-permute-start | bytes 1572872 | tf_op jit(solution)/shard_map/while/body/eval_jaxpr/ppermute | solution.py:12
  584.1 16.9 %collective-permute-start.3 = (bf16[128,2048]{0,1:T(8,128)(2,1)}, bf16[128,2048]{0,1:T(8,128)(2,1)S(1)}, u32[]{:S(2)}, u32[]{:S(2)}) collective-permute-start(bf16[128,2048]{0,1:T(8,128)(2,1)} %get-tuple-element.582), channel_id=1, source_target_pairs={{8,0},{16,8},{24,16},{32,24},{40,32},{48,40},{56,48},{64,56},{72,6... | collective-permute-start | bytes 1572872 | tf_op jit(solution)/shard_map/while/body/eval_jaxpr/ppermute | solution.py:12
  585.4 21.3 %collective-permute-start.2 = (bf16[128,2048]{0,1:T(8,128)(2,1)}, bf16[128,2048]{0,1:T(8,128)(2,1)}, u32[]{:S(2)}, u32[]{:S(2)}) collective-permute-start(bf16[128,2048]{0,1:T(8,128)(2,1)} %get-tuple-element.581), channel_id=1, source_target_pairs={{8,0},{16,8},{24,16},{32,24},{40,32},{48,40},{56,48},{64,56},{72,6... | collective-permute-start | bytes 1572872 | tf_op jit(solution)/shard_map/while/body/eval_jaxpr/ppermute | solution.py:12
  638.1 15.6 %collective-permute-start.3 = (bf16[128,2048]{0,1:T(8,128)(2,1)}, bf16[128,2048]{0,1:T(8,128)(2,1)S(1)}, u32[]{:S(2)}, u32[]{:S(2)}) collective-permute-start(bf16[128,2048]{0,1:T(8,128)(2,1)} %get-tuple-element.582), channel_id=1, source_target_pairs={{8,0},{16,8},{24,16},{32,24},{40,32},{48,40},{56,48},{64,56},{72,6... | collective-permute-start | bytes 1572872 | tf_op jit(solution)/shard_map/while/body/eval_jaxpr/ppermute | solution.py:12
  639.4 20.0 %collective-permute-start.2 = (bf16[128,2048]{0,1:T(8,128)(2,1)}, bf16[128,2048]{0,1:T(8,128)(2,1)}, u32[]{:S(2)}, u32[]{:S(2)}) collective-permute-start(bf16[128,2048]{0,1:T(8,128)(2,1)} %get-tuple-element.581), channel_id=1, source_target_pairs={{8,0},{16,8},{24,16},{32,24},{40,32},{48,40},{56,48},{64,56},{72,6... | collective-permute-start | bytes 1572872 | tf_op jit(solution)/shard_map/while/body/eval_jaxpr/ppermute | solution.py:12
  690.6 15.6 %collective-permute-start.3 = (bf16[128,2048]{0,1:T(8,128)(2,1)}, bf16[128,2048]{0,1:T(8,128)(2,1)S(1)}, u32[]{:S(2)}, u32[]{:S(2)}) collective-permute-start(bf16[128,2048]{0,1:T(8,128)(2,1)} %get-tuple-element.582), channel_id=1, source_target_pairs={{8,0},{16,8},{24,16},{32,24},{40,32},{48,40},{56,48},{64,56},{72,6... | collective-permute-start | bytes 1572872 | tf_op jit(solution)/shard_map/while/body/eval_jaxpr/ppermute | solution.py:12
  691.9 20.0 %collective-permute-start.2 = (bf16[128,2048]{0,1:T(8,128)(2,1)}, bf16[128,2048]{0,1:T(8,128)(2,1)}, u32[]{:S(2)}, u32[]{:S(2)}) collective-permute-start(bf16[128,2048]{0,1:T(8,128)(2,1)} %get-tuple-element.581), channel_id=1, source_target_pairs={{8,0},{16,8},{24,16},{32,24},{40,32},{48,40},{56,48},{64,56},{72,6... | collective-permute-start | bytes 1572872 | tf_op jit(solution)/shard_map/while/body/eval_jaxpr/ppermute | solution.py:12
  743.0 15.6 %collective-permute-start.3 = (bf16[128,2048]{0,1:T(8,128)(2,1)}, bf16[128,2048]{0,1:T(8,128)(2,1)S(1)}, u32[]{:S(2)}, u32[]{:S(2)}) collective-permute-start(bf16[128,2048]{0,1:T(8,128)(2,1)} %get-tuple-element.582), channel_id=1, source_target_pairs={{8,0},{16,8},{24,16},{32,24},{40,32},{48,40},{56,48},{64,56},{72,6... | collective-permute-start | bytes 1572872 | tf_op jit(solution)/shard_map/while/body/eval_jaxpr/ppermute | solution.py:12
  744.3 20.0 %collective-permute-start.2 = (bf16[128,2048]{0,1:T(8,128)(2,1)}, bf16[128,2048]{0,1:T(8,128)(2,1)}, u32[]{:S(2)}, u32[]{:S(2)}) collective-permute-start(bf16[128,2048]{0,1:T(8,128)(2,1)} %get-tuple-element.581), channel_id=1, source_target_pairs={{8,0},{16,8},{24,16},{32,24},{40,32},{48,40},{56,48},{64,56},{72,6... | collective-permute-start | bytes 1572872 | tf_op jit(solution)/shard_map/while/body/eval_jaxpr/ppermute | solution.py:12
  795.4 15.6 %collective-permute-start.3 = (bf16[128,2048]{0,1:T(8,128)(2,1)}, bf16[128,2048]{0,1:T(8,128)(2,1)S(1)}, u32[]{:S(2)}, u32[]{:S(2)}) collective-permute-start(bf16[128,2048]{0,1:T(8,128)(2,1)} %get-tuple-element.582), channel_id=1, source_target_pairs={{8,0},{16,8},{24,16},{32,24},{40,32},{48,40},{56,48},{64,56},{72,6... | collective-permute-start | bytes 1572872 | tf_op jit(solution)/shard_map/while/body/eval_jaxpr/ppermute | solution.py:12
  796.7 20.0 %collective-permute-start.2 = (bf16[128,2048]{0,1:T(8,128)(2,1)}, bf16[128,2048]{0,1:T(8,128)(2,1)}, u32[]{:S(2)}, u32[]{:S(2)}) collective-permute-start(bf16[128,2048]{0,1:T(8,128)(2,1)} %get-tuple-element.581), channel_id=1, source_target_pairs={{8,0},{16,8},{24,16},{32,24},{40,32},{48,40},{56,48},{64,56},{72,6... | collective-permute-start | bytes 1572872 | tf_op jit(solution)/shard_map/while/body/eval_jaxpr/ppermute | solution.py:12
  845.6 15.6 %collective-permute-start.3 = (bf16[128,2048]{0,1:T(8,128)(2,1)}, bf16[128,2048]{0,1:T(8,128)(2,1)S(1)}, u32[]{:S(2)}, u32[]{:S(2)}) collective-permute-start(bf16[128,2048]{0,1:T(8,128)(2,1)} %get-tuple-element.582), channel_id=1, source_target_pairs={{8,0},{16,8},{24,16},{32,24},{40,32},{48,40},{56,48},{64,56},{72,6... | collective-permute-start | bytes 1572872 | tf_op jit(solution)/shard_map/while/body/eval_jaxpr/ppermute | solution.py:12
  846.9 20.0 %collective-permute-start.2 = (bf16[128,2048]{0,1:T(8,128)(2,1)}, bf16[128,2048]{0,1:T(8,128)(2,1)}, u32[]{:S(2)}, u32[]{:S(2)}) collective-permute-start(bf16[128,2048]{0,1:T(8,128)(2,1)} %get-tuple-element.581), channel_id=1, source_target_pairs={{8,0},{16,8},{24,16},{32,24},{40,32},{48,40},{56,48},{64,56},{72,6... | collective-permute-start | bytes 1572872 | tf_op jit(solution)/shard_map/while/body/eval_jaxpr/ppermute | solution.py:12
  (155 other events, 782.1 us)
where the time goes:
time: 897 us; the launch traced here: 889 us
  waiting for transfers between devices  325 us (36%)
  starting transfers between devices  235 us (26%)
  local copies, waits for them, and re-layouts  146 us (16%)
  other arithmetic  95.9 us (11%)
  matrix products  83.6 us (9%)
    ppermute x90, waiting for transfers between devices, shifted(): lax.ppermute(value, axis, [(source, source + steps) for source in range(f...  325 us
    ppermute x90, starting transfers between devices, shifted(): lax.ppermute(value, axis, [(source, source + steps) for source in range(f...  235 us
    while x240, local copies, waits for them, and re-layouts  107 us
    dot_general x16, matrix products, key_value_terms(): jnp.einsum('hqk,qhd->khd', dscores_low, head_view(query), preferred_eleme...  47.9 us
    add x15, other arithmetic, advance(): key_acc + key_part  36 us
    add x15, other arithmetic, advance(): query_acc = query_acc + lax.cond(source >= 0, own_queries, lambda: empty)  34.5 us
    dot_general x16, matrix products, score_grads(): jnp.einsum('qhd,khd->hqk', head_view(query), head_view(key_rows), preferr...  26.8 us
    mul x16, local copies, waits for them, and re-layouts, key_value_terms(): key_part.reshape(rows, -1) * HD ** (-0.5)  24.7 us
  transfers between devices with their start and end apart: 90, of which 63 were waited for; matrix products, arithmetic and copies ran while one was open for 4% of the time, Pallas kernels for 0%

commit v1 on v0

v1 whole, which is shorter than its diff:
```python
import functools
import math

import jax
import jax.numpy as jnp
from jax import lax
from jax.experimental import pallas as pl
from jax.experimental.pallas import tpu as pltpu
from jax.sharding import PartitionSpec as P

HD = 128
SCALE = HD**-0.5
LOG2E = math.log2(math.e)
STATS = 16
TILE = 256
VMEM_LIMIT = 48 * 1024 * 1024

NT = (((1,), (1,)), ((), ()))
NN = (((1,), (0,)), ((), ()))


def dot(left, right, dims):
    return lax.dot_general(left, right, dims, preferred_element_type=jnp.float32)


def vmem_specs(count):
    return [pl.BlockSpec(memory_space=pltpu.VMEM)] * count


def pack_kernel(q_ref, k_ref, v_ref, o_ref, g_ref, lse_ref, send_ref):
    heads = send_ref.shape[0]
    rows = q_ref.shape[0]
    ones = jnp.ones((STATS, HD), jnp.bfloat16)
    which = lax.broadcasted_iota(jnp.int32, (STATS, rows), 0)
    for head in range(heads):
        cols = slice(head * HD, (head + 1) * HD)
        for place, ref in enumerate((q_ref, k_ref, v_ref, g_ref)):
            send_ref[head, place * rows : (place + 1) * rows, :] = ref[:, cols]
        product = g_ref[:, cols].astype(jnp.float32) * o_ref[:, cols].astype(jnp.float32)
        high = product.astype(jnp.bfloat16)
        low = (product - high.astype(jnp.float32)).astype(jnp.bfloat16)
        delta = dot(ones, high, NT) + dot(ones, low, NT)
        delta_high = delta.astype(jnp.bfloat16).astype(jnp.float32)
        delta_low = delta - delta_high
        lse = lse_ref[head : head + 1, :].astype(jnp.float32)
        stats = jnp.where(which == 0, lse, jnp.where(which == 1, delta_high, delta_low))
        send_ref[head, 4 * rows :, :] = stats.astype(jnp.bfloat16)


def head_kernel(x_ref, out_ref, p_ref, ds_ref, kt_ref, lse_ref, delta_ref):
    blocks = x_ref.shape[0]
    rows = HD
    tokens = blocks * rows

    def piece(place, start, count):
        part = x_ref[start // rows : (start + count) // rows, place * rows : (place + 1) * rows, :]
        return part.reshape(count, HD)

    def put(place, start, value):
        for step in range(value.shape[0] // rows):
            part = value[step * rows : (step + 1) * rows].astype(jnp.bfloat16)
            out_ref[start // rows + step, place * rows : (place + 1) * rows, :] = part

    for block in range(blocks):
        cols = slice(block * rows, (block + 1) * rows)
        stats = x_ref[block, 4 * rows :, :].astype(jnp.float32)
        lse_ref[:, cols] = jnp.broadcast_to(stats[0:1] * LOG2E, (8, rows))
        delta_ref[:, cols] = jnp.broadcast_to(stats[1:2] + stats[2:3], (8, rows))
        kt_ref[:, cols] = x_ref[block, rows : 2 * rows, :].T

    for key_start in range(0, tokens, TILE):
        keys = piece(1, key_start, TILE)
        values = piece(2, key_start, TILE)
        key_rows = slice(key_start, key_start + TILE)
        for start in range(key_start, tokens, TILE):
            cols = slice(start, start + TILE)
            scores = dot(keys, piece(0, start, TILE), NT)
            dprobs = dot(values, piece(3, start, TILE), NT)
            probs = jnp.exp2(scores * (SCALE * LOG2E) - lse_ref[0:1, cols])
            if start == key_start:
                key_pos = lax.broadcasted_iota(jnp.int32, (TILE, TILE), 0)
                query_pos = lax.broadcasted_iota(jnp.int32, (TILE, TILE), 1)
                probs = jnp.where(key_pos <= query_pos, probs, 0.0)
            dscores = probs * (dprobs - delta_ref[0:1, cols])
            p_ref[key_rows, cols] = probs.astype(jnp.bfloat16)
            ds_ref[key_rows, cols] = dscores.astype(jnp.bfloat16)
        count = tokens - key_start
        put(1, key_start, dot(ds_ref[key_rows, key_start:], piece(0, key_start, count), NN) * SCALE)
        put(2, key_start, dot(p_ref[key_rows, key_start:], piece(3, key_start, count), NN))
    for start in range(0, tokens, TILE):
        stop = start + TILE
        query_grad = dot(kt_ref[:, :stop], ds_ref[:stop, start:stop], NN)
        put(0, start, query_grad.T * SCALE)


def unpack_kernel(recv_ref, dq_ref, dk_ref, dv_ref):
    rows = dq_ref.shape[0]
    for head in range(recv_ref.shape[0]):
        cols = slice(head * HD, (head + 1) * HD)
        for place, ref in enumerate((dq_ref, dk_ref, dv_ref)):
            ref[:, cols] = recv_ref[head, place * rows : (place + 1) * rows, :]


def call(kernel, ins, outs, scratch=()):
    return pl.pallas_call(
        kernel,
        out_shape=outs,
        in_specs=vmem_specs(ins),
        out_specs=jax.tree.map(lambda _: vmem_specs(1)[0], outs),
        scratch_shapes=scratch,
        compiler_params=pltpu.CompilerParams(vmem_limit_bytes=VMEM_LIMIT),
    )


def local(queries, keys, values, outputs, out_grad, log_norm):
    rows, width = queries.shape
    heads = width // HD
    tokens = rows * lax.axis_size("ctx")
    bf16 = functools.partial(jax.ShapeDtypeStruct, dtype=jnp.bfloat16)
    with jax.named_scope("pack"):
        send = call(pack_kernel, 6, bf16((heads, 4 * rows + STATS, HD)))(
            queries, keys, values, outputs, out_grad, log_norm
        )
    with jax.named_scope("to_heads"):
        x = lax.all_to_all(send, "ctx", 0, 0, tiled=True)
    with jax.named_scope("head_grads"):
        scratch = (
            pltpu.VMEM((tokens, tokens), jnp.bfloat16),
            pltpu.VMEM((tokens, tokens), jnp.bfloat16),
            pltpu.VMEM((HD, tokens), jnp.bfloat16),
            pltpu.VMEM((8, tokens), jnp.float32),
            pltpu.VMEM((8, tokens), jnp.float32),
        )
        grads = call(head_kernel, 1, bf16((heads, 3 * rows, HD)), scratch)(x)
    with jax.named_scope("to_tokens"):
        back = lax.all_to_all(grads, "ctx", 0, 0, tiled=True)
    with jax.named_scope("unpack"):
        return call(unpack_kernel, 1, (bf16((rows, width)),) * 3)(back)


def solution(mesh):
    tokens = P(("doc", "ctx"), None)
    in_specs = (tokens,) * 5 + (P(None, ("doc", "ctx")),)
    return jax.shard_map(
        local, mesh=mesh, in_specs=in_specs, out_specs=(tokens,) * 3, check_vma=False
    )
```

time: 897 us -> 77.7 us (0.09)
  waiting for transfers between devices: 325 us -> 0 us
  starting transfers between devices: 235 us -> 0 us
  local copies, waits for them, and re-layouts: 146 us -> 5.89 us
  other arithmetic: 95.9 us -> 0 us
  matrix products: 83.6 us -> 0 us
  blocking collectives: 0 us -> 62.2 us
    ppermute x90 -> x0, waiting for transfers between devices: 325 us -> none  [shifted(): lax.ppermute(value, axis, [(source, source + steps) for source in range(f...]
    ppermute x90 -> x0, starting transfers between devices: 235 us -> none  [shifted(): lax.ppermute(value, axis, [(source, source + steps) for source in range(f...]
    while x247 -> x0, local copies, waits for them, and re-layouts: 115 us -> none
    dot_general x50 -> x0, matrix products: 83.6 us -> none  [the longest x16 47.9 us: key_value_terms(): jnp.einsum('hqk,qhd->khd', dscores_low, head_view(query), preferred_eleme...]
    add x61 -> x0, other arithmetic: 74 us -> none  [the longest x15 36 us: advance(): key_acc + key_part]
    all_to_all x0 -> x2, blocking collectives: none -> 62.2 us  [the longest x1 36.9 us: local(): x = lax.all_to_all(send, 'ctx', 0, 0, tiled=True)]
    mul x17 -> x0, local copies, waits for them, and re-layouts: 26 us -> none  [the longest x16 24.7 us: key_value_terms(): key_part.reshape(rows, -1) * HD ** (-0.5)]
    reduce_sum x16 -> x0, other arithmetic: 20.4 us -> none  [row_delta(): return jnp.sum(product.reshape(grad_rows.shape[0], -1, HD), -1).T]
  transfers between devices with their start and end apart: 90 -> 0, of which waited for: 63 -> 0; matrix products, arithmetic and copies ran while one was open for 4% -> 0% of each run, Pallas kernels for 0% -> 0%
where the time goes in v1:
time: 77.7 us; the launch traced here: 77.3 us
  blocking collectives  62.2 us (80%)
  Pallas kernels  8.51 us (11%)
  local copies, waits for them, and re-layouts  5.89 us (8%)
    all_to_all x1, blocking collectives, local(): x = lax.all_to_all(send, 'ctx', 0, 0, tiled=True)  36.9 us
    all_to_all x1, blocking collectives, local(): back = lax.all_to_all(grads, 'ctx', 0, 0, tiled=True)  25.3 us
    pallas_call x1, Pallas kernels, local(): grads = call(head_kernel, 1, bf16((heads, 3 * rows, HD)), scratch)(x)  6.03 us
    unnamed x12, local copies, waits for them, and re-layouts  5.89 us
    pallas_call x1, Pallas kernels, local(): return call(unpack_kernel, 1, (bf16((rows, width)),) * 3)(back)  1.57 us

profile of v1, /device:TPU:0, one launch (start us, length us, event | category | flops | bytes accessed | tf_op | source)
XLA Modules:
  0.0 77.3 jit_solution(6054923621797610032)
XLA Ops:
  0.6 0.0 copy-start
  0.6 1.0 %copy-done = bf16[128,2048]{1,0:T(8,128)(2,1)S(1)} copy-done((bf16[128,2048]{1,0:T(8,128)(2,1)S(1)}, bf16[128,2048]{1,0:T(8,128)(2,1)}, u32[]{:S(2)}) %copy-start) | copy-done | bytes 524312
  1.7 0.0 copy-start.1
  1.7 1.0 %copy-done.1 = bf16[128,2048]{1,0:T(8,128)(2,1)S(1)} copy-done((bf16[128,2048]{1,0:T(8,128)(2,1)S(1)}, bf16[128,2048]{1,0:T(8,128)(2,1)}, u32[]{:S(2)}) %copy-start.1) | copy-done | bytes 524312
  2.7 0.0 copy-start.2
  2.7 1.0 %copy-done.2 = bf16[128,2048]{1,0:T(8,128)(2,1)S(1)} copy-done((bf16[128,2048]{1,0:T(8,128)(2,1)S(1)}, bf16[128,2048]{1,0:T(8,128)(2,1)}, u32[]{:S(2)}) %copy-start.2) | copy-done | bytes 524312
  3.8 0.0 copy-start.3
  3.8 1.0 %copy-done.3 = bf16[128,2048]{1,0:T(8,128)(2,1)S(1)} copy-done((bf16[128,2048]{1,0:T(8,128)(2,1)S(1)}, bf16[128,2048]{1,0:T(8,128)(2,1)}, u32[]{:S(2)}) %copy-start.3) | copy-done | bytes 524312
  4.8 0.0 copy-start.4
  4.8 1.0 %copy-done.4 = bf16[128,2048]{1,0:T(8,128)(2,1)S(1)} copy-done((bf16[128,2048]{1,0:T(8,128)(2,1)S(1)}, bf16[128,2048]{1,0:T(8,128)(2,1)}, u32[]{:S(2)}) %copy-start.4) | copy-done | bytes 524312
  5.8 0.0 copy-start.5
  5.8 0.7 copy-done.5
  6.5 0.9 %pack.1 = bf16[16,528,128]{2,1,0:T(8,128)(2,1)S(1)} custom-call(bf16[128,2048]{1,0:T(8,128)(2,1)S(1)} %copy-done, bf16[128,2048]{1,0:T(8,128)(2,1)S(1)} %copy-done.1, bf16[128,2048]{1,0:T(8,128)(2,1)S(1)} %copy-done.2, bf16[128,2048]{1,0:T(8,128)(2,1)S(1)} %copy-done.3, bf16[128,2048]{1,0:T(8,128)(2,1)S(1)} %copy-done.4, bf16[16,128]{1,0:T(8,128)(2,1)S(1)} %copy-done.5), custom_call_target="tpu_custom_call" | custom-call | tf_op jit(solution)/shard_map/pack/pallas_call | solution.py:121
  7.4 36.9 %all_to_all.10.x_ref = bf16[16,528,128]{2,1,0:T(8,128)(2,1)S(1)} all-to-all(bf16[16,528,128]{2,1,0:T(8,128)(2,1)S(1)} %pack.1), channel_id=1, replica_groups=mesh['ctx'=16,'doc'=8] {'ctx'}, dimensions={0} | all-to-all | bytes 4325376 | tf_op jit(solution)/shard_map/to_heads/all_to_all | solution.py:125
  44.3 6.0 %head_grads.1 = bf16[16,384,128]{2,1,0:T(8,128)(2,1)S(1)} custom-call(bf16[16,528,128]{2,1,0:T(8,128)(2,1)S(1)} %all_to_all.10.x_ref), custom_call_target="tpu_custom_call" | custom-call | tf_op jit(solution)/shard_map/head_grads/pallas_call | solution.py:134
  50.4 25.3 %all_to_all.11.recv_ref = bf16[16,384,128]{2,1,0:T(8,128)(2,1)S(1)} all-to-all(bf16[16,384,128]{2,1,0:T(8,128)(2,1)S(1)} %head_grads.1), channel_id=1, replica_groups=mesh['ctx'=16,'doc'=8] {'ctx'}, dimensions={0} | all-to-all | bytes 3145728 | tf_op jit(solution)/shard_map/to_tokens/all_to_all | solution.py:136
  75.7 1.6 %unpack.1 = (bf16[128,2048]{1,0:T(8,128)(2,1)}, bf16[128,2048]{1,0:T(8,128)(2,1)}, bf16[128,2048]{1,0:T(8,128)(2,1)}) custom-call(bf16[16,384,128]{2,1,0:T(8,128)(2,1)S(1)} %all_to_all.11.recv_ref), custom_call_target="tpu_custom_call" | custom-call | tf_op jit(solution)/shard_map/unpack/pallas_call | solution.py:138
Async XLA Ops:
  0.6 1.0 %copy-start = (bf16[128,2048]{1,0:T(8,128)(2,1)S(1)}, bf16[128,2048]{1,0:T(8,128)(2,1)}, u32[]{:S(2)}) copy-start(bf16[128,2048]{1,0:T(8,128)(2,1)} %q_ref.1) | copy-start | bytes 1572868
  1.7 1.0 %copy-start.1 = (bf16[128,2048]{1,0:T(8,128)(2,1)S(1)}, bf16[128,2048]{1,0:T(8,128)(2,1)}, u32[]{:S(2)}) copy-start(bf16[128,2048]{1,0:T(8,128)(2,1)} %k_ref.1) | copy-start | bytes 1572868
  2.7 1.0 %copy-start.2 = (bf16[128,2048]{1,0:T(8,128)(2,1)S(1)}, bf16[128,2048]{1,0:T(8,128)(2,1)}, u32[]{:S(2)}) copy-start(bf16[128,2048]{1,0:T(8,128)(2,1)} %v_ref.1) | copy-start | bytes 1572868
  3.8 1.0 %copy-start.3 = (bf16[128,2048]{1,0:T(8,128)(2,1)S(1)}, bf16[128,2048]{1,0:T(8,128)(2,1)}, u32[]{:S(2)}) copy-start(bf16[128,2048]{1,0:T(8,128)(2,1)} %o_ref.1) | copy-start | bytes 1572868
  4.8 1.0 %copy-start.4 = (bf16[128,2048]{1,0:T(8,128)(2,1)S(1)}, bf16[128,2048]{1,0:T(8,128)(2,1)}, u32[]{:S(2)}) copy-start(bf16[128,2048]{1,0:T(8,128)(2,1)} %g_ref.1) | copy-start | bytes 1572868
  5.8 0.7 copy-start.5

commit v2 on v1

--- a/solution.py
+++ b/solution.py
@@ -23,28 +23,42 @@
     return lax.dot_general(left, right, dims, preferred_element_type=jnp.float32)
 
 
-def vmem_specs(count):
-    return [pl.BlockSpec(memory_space=pltpu.VMEM)] * count
-
-
-def pack_kernel(q_ref, k_ref, v_ref, o_ref, g_ref, lse_ref, send_ref):
+def pack_kernel(q_ref, k_ref, v_ref, o_ref, g_ref, lse_ref, send_ref, o_buf, lse_buf, sems):
     heads = send_ref.shape[0]
     rows = q_ref.shape[0]
+    own = (
+        pltpu.make_async_copy(o_ref, o_buf, sems.at[4]),
+        pltpu.make_async_copy(lse_ref, lse_buf, sems.at[5]),
+    )
+    for copy in own:
+        copy.start()
+    sources = (q_ref, k_ref, v_ref, g_ref)
+    for place in (3, 0, 1, 2):
+        for head in range(heads):
+            pltpu.make_async_copy(
+                sources[place].at[:, head * HD : (head + 1) * HD],
+                send_ref.at[head, place * rows : (place + 1) * rows, :],
+                sems.at[place],
+            ).start()
+    for copy in own:
+        copy.wait()
+    pltpu.make_async_copy(g_ref, g_ref, sems.at[3]).wait()
     ones = jnp.ones((STATS, HD), jnp.bfloat16)
     which = lax.broadcasted_iota(jnp.int32, (STATS, rows), 0)
     for head in range(heads):
         cols = slice(head * HD, (head + 1) * HD)
-        for place, ref in enumerate((q_ref, k_ref, v_ref, g_ref)):
-            send_ref[head, place * rows : (place + 1) * rows, :] = ref[:, cols]
-        product = g_ref[:, cols].astype(jnp.float32) * o_ref[:, cols].astype(jnp.float32)
+        grads = send_ref[head, 3 * rows : 4 * rows, :]
+        product = grads.astype(jnp.float32) * o_buf[:, cols].astype(jnp.float32)
         high = product.astype(jnp.bfloat16)
         low = (product - high.astype(jnp.float32)).astype(jnp.bfloat16)
         delta = dot(ones, high, NT) + dot(ones, low, NT)
         delta_high = delta.astype(jnp.bfloat16).astype(jnp.float32)
         delta_low = delta - delta_high
-        lse = lse_ref[head : head + 1, :].astype(jnp.float32)
+        lse = lse_buf[head : head + 1, :].astype(jnp.float32)
         stats = jnp.where(which == 0, lse, jnp.where(which == 1, delta_high, delta_low))
         send_ref[head, 4 * rows :, :] = stats.astype(jnp.bfloat16)
+    for place in range(3):
+        pltpu.make_async_copy(sources[place], sources[place], sems.at[place]).wait()
 
 
 def head_kernel(x_ref, out_ref, p_ref, ds_ref, kt_ref, lse_ref, delta_ref):
@@ -93,20 +107,30 @@
         put(0, start, query_grad.T * SCALE)
 
 
-def unpack_kernel(recv_ref, dq_ref, dk_ref, dv_ref):
+def unpack_kernel(recv_ref, dq_ref, dk_ref, dv_ref, sems):
     rows = dq_ref.shape[0]
-    for head in range(recv_ref.shape[0]):
-        cols = slice(head * HD, (head + 1) * HD)
-        for place, ref in enumerate((dq_ref, dk_ref, dv_ref)):
-            ref[:, cols] = recv_ref[head, place * rows : (place + 1) * rows, :]
+    outs = (dq_ref, dk_ref, dv_ref)
+    for place, ref in enumerate(outs):
+        for head in range(recv_ref.shape[0]):
+            pltpu.make_async_copy(
+                recv_ref.at[head, place * rows : (place + 1) * rows, :],
+                ref.at[:, head * HD : (head + 1) * HD],
+                sems.at[place],
+            ).start()
+    for place, ref in enumerate(outs):
+        pltpu.make_async_copy(ref, ref, sems.at[place]).wait()
 
 
-def call(kernel, ins, outs, scratch=()):
+IN_HBM = pl.BlockSpec(memory_space=pl.ANY)
+IN_VMEM = pl.BlockSpec(memory_space=pltpu.VMEM)
+
+
+def call(kernel, ins, outs, out_specs, scratch):
     return pl.pallas_call(
         kernel,
         out_shape=outs,
-        in_specs=vmem_specs(ins),
-        out_specs=jax.tree.map(lambda _: vmem_specs(1)[0], outs),
+        in_specs=ins,
+        out_specs=out_specs,
         scratch_shapes=scratch,
         compiler_params=pltpu.CompilerParams(vmem_limit_bytes=VMEM_LIMIT),
     )
@@ -118,7 +142,13 @@
     tokens = rows * lax.axis_size("ctx")
     bf16 = functools.partial(jax.ShapeDtypeStruct, dtype=jnp.bfloat16)
     with jax.named_scope("pack"):
-        send = call(pack_kernel, 6, bf16((heads, 4 * rows + STATS, HD)))(
+        scratch = (
+            pltpu.VMEM((rows, width), jnp.bfloat16),
+            pltpu.VMEM((heads, rows), jnp.bfloat16),
+            pltpu.SemaphoreType.DMA((6,)),
+        )
+        shape = bf16((heads, 4 * rows + STATS, HD))
+        send = call(pack_kernel, [IN_HBM] * 6, shape, IN_VMEM, scratch)(
             queries, keys, values, outputs, out_grad, log_norm
         )
     with jax.named_scope("to_heads"):
@@ -131,11 +161,14 @@
             pltpu.VMEM((8, tokens), jnp.float32),
             pltpu.VMEM((8, tokens), jnp.float32),
         )
-        grads = call(head_kernel, 1, bf16((heads, 3 * rows, HD)), scratch)(x)
+        shape = bf16((heads, 3 * rows, HD))
+        grads = call(head_kernel, [IN_VMEM], shape, IN_VMEM, scratch)(x)
     with jax.named_scope("to_tokens"):
         back = lax.all_to_all(grads, "ctx", 0, 0, tiled=True)
     with jax.named_scope("unpack"):
-        return call(unpack_kernel, 1, (bf16((rows, width)),) * 3)(back)
+        shapes = (bf16((rows, width)),) * 3
+        scratch = (pltpu.SemaphoreType.DMA((3,)),)
+        return call(unpack_kernel, [IN_VMEM], shapes, (IN_HBM,) * 3, scratch)(back)
 
 
 def solution(mesh):

time: 77.7 us -> 77.7 us (level)
  no operation moved by 1% of the time
where the time goes in v2:
time: 77.7 us; the launch traced here: 77.3 us
  blocking collectives  62.2 us (80%)
  Pallas kernels  8.51 us (11%)
  local copies, waits for them, and re-layouts  5.89 us (8%)
    all_to_all x1, blocking collectives, local(): x = lax.all_to_all(send, 'ctx', 0, 0, tiled=True)  36.9 us
    all_to_all x1, blocking collectives, local(): back = lax.all_to_all(grads, 'ctx', 0, 0, tiled=True)  25.3 us
    pallas_call x1, Pallas kernels, local(): grads = call(head_kernel, [IN_VMEM], shape, IN_VMEM, scratch)(x)  6.03 us
    unnamed x12, local copies, waits for them, and re-layouts  5.89 us

profile of v2, /device:TPU:0, one launch (start us, length us, event | category | flops | bytes accessed | tf_op | source)
XLA Modules:
  0.0 77.3 jit_solution(12964907081418978156)
XLA Ops:
  0.6 0.0 copy-start
  0.6 1.0 %copy-done = bf16[128,2048]{1,0:T(8,128)(2,1)S(1)} copy-done((bf16[128,2048]{1,0:T(8,128)(2,1)S(1)}, bf16[128,2048]{1,0:T(8,128)(2,1)}, u32[]{:S(2)}) %copy-start) | copy-done | bytes 524312
  1.7 0.0 copy-start.1
  1.7 1.0 %copy-done.1 = bf16[128,2048]{1,0:T(8,128)(2,1)S(1)} copy-done((bf16[128,2048]{1,0:T(8,128)(2,1)S(1)}, bf16[128,2048]{1,0:T(8,128)(2,1)}, u32[]{:S(2)}) %copy-start.1) | copy-done | bytes 524312
  2.7 0.0 copy-start.2
  2.7 1.0 %copy-done.2 = bf16[128,2048]{1,0:T(8,128)(2,1)S(1)} copy-done((bf16[128,2048]{1,0:T(8,128)(2,1)S(1)}, bf16[128,2048]{1,0:T(8,128)(2,1)}, u32[]{:S(2)}) %copy-start.2) | copy-done | bytes 524312
  3.8 0.0 copy-start.3
  3.8 1.0 %copy-done.3 = bf16[128,2048]{1,0:T(8,128)(2,1)S(1)} copy-done((bf16[128,2048]{1,0:T(8,128)(2,1)S(1)}, bf16[128,2048]{1,0:T(8,128)(2,1)}, u32[]{:S(2)}) %copy-start.3) | copy-done | bytes 524312
  4.8 0.0 copy-start.4
  4.8 1.0 %copy-done.4 = bf16[128,2048]{1,0:T(8,128)(2,1)S(1)} copy-done((bf16[128,2048]{1,0:T(8,128)(2,1)S(1)}, bf16[128,2048]{1,0:T(8,128)(2,1)}, u32[]{:S(2)}) %copy-start.4) | copy-done | bytes 524312
  5.8 0.0 copy-start.5
  5.8 0.7 copy-done.5
  6.5 1.3 %pack.1 = bf16[16,528,128]{2,1,0:T(8,128)(2,1)S(1)} custom-call(bf16[128,2048]{1,0:T(8,128)(2,1)S(1)} %copy-done, bf16[128,2048]{1,0:T(8,128)(2,1)S(1)} %copy-done.1, bf16[128,2048]{1,0:T(8,128)(2,1)S(1)} %copy-done.2, bf16[128,2048]{1,0:T(8,128)(2,1)S(1)} %copy-done.3, bf16[128,2048]{1,0:T(8,128)(2,1)S(1)} %copy-done.4, bf16[16,128]{1,0:T(8,128)(2,1)S(1)} %copy-done.5), custom_call_target="tpu_custom_call" | custom-call | tf_op jit(solution)/shard_map/pack/pallas_call | solution.py:151
  7.9 36.9 %all_to_all.10.x_ref = bf16[16,528,128]{2,1,0:T(8,128)(2,1)S(1)} all-to-all(bf16[16,528,128]{2,1,0:T(8,128)(2,1)S(1)} %pack.1), channel_id=1, replica_groups=mesh['ctx'=16,'doc'=8] {'ctx'}, dimensions={0} | all-to-all | bytes 4325376 | tf_op jit(solution)/shard_map/to_heads/all_to_all | solution.py:155
  44.8 6.0 %head_grads.1 = bf16[16,384,128]{2,1,0:T(8,128)(2,1)S(1)} custom-call(bf16[16,528,128]{2,1,0:T(8,128)(2,1)S(1)} %all_to_all.10.x_ref), custom_call_target="tpu_custom_call" | custom-call | tf_op jit(solution)/shard_map/head_grads/pallas_call | solution.py:165
  50.8 25.3 %all_to_all.11.recv_ref = bf16[16,384,128]{2,1,0:T(8,128)(2,1)S(1)} all-to-all(bf16[16,384,128]{2,1,0:T(8,128)(2,1)S(1)} %head_grads.1), channel_id=1, replica_groups=mesh['ctx'=16,'doc'=8] {'ctx'}, dimensions={0} | all-to-all | bytes 3145728 | tf_op jit(solution)/shard_map/to_tokens/all_to_all | solution.py:167
  76.1 1.1 %unpack.1 = (bf16[128,2048]{1,0:T(8,128)(2,1)}, bf16[128,2048]{1,0:T(8,128)(2,1)}, bf16[128,2048]{1,0:T(8,128)(2,1)}) custom-call(bf16[16,384,128]{2,1,0:T(8,128)(2,1)S(1)} %all_to_all.11.recv_ref), custom_call_target="tpu_custom_call" | custom-call | tf_op jit(solution)/shard_map/unpack/pallas_call | solution.py:171
Async XLA Ops:
  0.6 1.0 %copy-start = (bf16[128,2048]{1,0:T(8,128)(2,1)S(1)}, bf16[128,2048]{1,0:T(8,128)(2,1)}, u32[]{:S(2)}) copy-start(bf16[128,2048]{1,0:T(8,128)(2,1)} %q_ref.1) | copy-start | bytes 1572868
  1.7 1.0 %copy-start.1 = (bf16[128,2048]{1,0:T(8,128)(2,1)S(1)}, bf16[128,2048]{1,0:T(8,128)(2,1)}, u32[]{:S(2)}) copy-start(bf16[128,2048]{1,0:T(8,128)(2,1)} %k_ref.1) | copy-start | bytes 1572868
  2.7 1.0 %copy-start.2 = (bf16[128,2048]{1,0:T(8,128)(2,1)S(1)}, bf16[128,2048]{1,0:T(8,128)(2,1)}, u32[]{:S(2)}) copy-start(bf16[128,2048]{1,0:T(8,128)(2,1)} %v_ref.1) | copy-start | bytes 1572868
  3.8 1.0 %copy-start.3 = (bf16[128,2048]{1,0:T(8,128)(2,1)S(1)}, bf16[128,2048]{1,0:T(8,128)(2,1)}, u32[]{:S(2)}) copy-start(bf16[128,2048]{1,0:T(8,128)(2,1)} %o_ref.1) | copy-start | bytes 1572868
  4.8 1.0 %copy-start.4 = (bf16[128,2048]{1,0:T(8,128)(2,1)S(1)}, bf16[128,2048]{1,0:T(8,128)(2,1)}, u32[]{:S(2)}) copy-start(bf16[128,2048]{1,0:T(8,128)(2,1)} %g_ref.1) | copy-start | bytes 1572868
  5.8 0.7 copy-start.5

commit v3 on v1

v3 whole, which is shorter than its diff:
```python
import functools
import math

import jax
import jax.numpy as jnp
from jax import lax
from jax.experimental import pallas as pl
from jax.experimental.pallas import tpu as pltpu
from jax.sharding import PartitionSpec as P

HD = 128
SCALE = HD**-0.5
LOG2E = math.log2(math.e)
STATS = 16
TILE = 256
HEAD_LIMIT = 48 * 1024 * 1024
PACK_LIMIT = 60 * 1024 * 1024

NT = (((1,), (1,)), ((), ()))
NN = (((1,), (0,)), ((), ()))

IN_HBM = pl.BlockSpec(memory_space=pltpu.HBM)
IN_VMEM = pl.BlockSpec(memory_space=pltpu.VMEM)


def dot(left, right, dims):
    return lax.dot_general(left, right, dims, preferred_element_type=jnp.float32)


def row_stats(grads, outs, lse):
    product = grads.astype(jnp.float32) * outs.astype(jnp.float32)
    high = product.astype(jnp.bfloat16)
    low = (product - high.astype(jnp.float32)).astype(jnp.bfloat16)
    ones = jnp.ones((STATS, HD), jnp.bfloat16)
    delta = dot(ones, high, NT) + dot(ones, low, NT)
    delta_high = delta.astype(jnp.bfloat16).astype(jnp.float32)
    which = lax.broadcasted_iota(jnp.int32, delta.shape, 0)
    stats = jnp.where(which == 1, delta_high, delta - delta_high)
    return jnp.where(which == 0, lse.astype(jnp.float32), stats).astype(jnp.bfloat16)


def pack_kernel(count, stats, *refs):
    total = max((count, *(place + 1 for place in stats)))
    sources, send_ref, held = refs[:total], refs[total], refs[total + 1 : 2 * total + 1]
    image, in_sems, out_sems = refs[2 * total + 1 :]
    heads = send_ref.shape[0]
    rows = sources[0].shape[0]

    def out(place):
        part = slice(place * rows, (place + 1) * rows if place < count else send_ref.shape[1])
        return pltpu.make_async_copy(
            image.at[:, part, :], send_ref.at[:, part, :], out_sems.at[place]
        )

    copies = [
        pltpu.make_async_copy(source, buffer, in_sems.at[place])
        for place, (source, buffer) in enumerate(zip(sources, held, strict=True))
    ]
    for copy in copies:
        copy.start()
    for place in range(count):
        copies[place].wait()
        for head in range(heads):
            image[head, place * rows : (place + 1) * rows, :] = held[place][
                :, head * HD : (head + 1) * HD
            ]
        out(place).start()
    if stats:
        for place in range(count, total):
            copies[place].wait()
        grads, outs, lse = (held[place] for place in stats)
        for head in range(heads):
            cols = slice(head * HD, (head + 1) * HD)
            image[head, count * rows :, :] = row_stats(
                grads[:, cols], outs[:, cols], lse[head : head + 1, :]
            )
        out(count).start()
    for place in range(count + bool(stats)):
        out(place).wait()


def head_kernel(layout, count, *refs):
    received, refs = refs[:count], refs[count:]
    out_ref, p_ref, ds_ref, kt_ref, lse_ref, delta_ref = refs
    blocks = out_ref.shape[0]
    rows = out_ref.shape[1] // 3
    tokens = blocks * rows

    def piece(name, start, count):
        which, at = layout[name]
        part = received[which][start // rows : (start + count) // rows, at : at + rows, :]
        return part.reshape(count, HD)

    def put(place, start, value):
        for step in range(value.shape[0] // rows):
            part = value[step * rows : (step + 1) * rows].astype(jnp.bfloat16)
            out_ref[start // rows + step, place * rows : (place + 1) * rows, :] = part

    for block in range(blocks):
        cols = slice(block * rows, (block + 1) * rows)
        which, at = layout["stats"]
        stats = received[which][block, at : at + STATS, :].astype(jnp.float32)
        lse_ref[:, cols] = jnp.broadcast_to(stats[0:1] * LOG2E, (8, rows))
        delta_ref[:, cols] = jnp.broadcast_to(stats[1:2] + stats[2:3], (8, rows))
        kt_ref[:, cols] = piece("k", block * rows, rows).T

    for key_start in range(0, tokens, TILE):
        keys = piece("k", key_start, TILE)
        values = piece("v", key_start, TILE)
        key_rows = slice(key_start, key_start + TILE)
        for start in range(key_start, tokens, TILE):
            cols = slice(start, start + TILE)
            scores = dot(keys, piece("q", start, TILE), NT)
            dprobs = dot(values, piece("g", start, TILE), NT)
            probs = jnp.exp2(scores * (SCALE * LOG2E) - lse_ref[0:1, cols])
            if start == key_start:
                key_pos = lax.broadcasted_iota(jnp.int32, (TILE, TILE), 0)
                query_pos = lax.broadcasted_iota(jnp.int32, (TILE, TILE), 1)
                probs = jnp.where(key_pos <= query_pos, probs, 0.0)
            dscores = probs * (dprobs - delta_ref[0:1, cols])
            p_ref[key_rows, cols] = probs.astype(jnp.bfloat16)
            ds_ref[key_rows, cols] = dscores.astype(jnp.bfloat16)
        rest = tokens - key_start
        put(1, key_start, dot(ds_ref[key_rows, key_start:], piece("q", key_start, rest), NN) * SCALE)
        put(2, key_start, dot(p_ref[key_rows, key_start:], piece("g", key_start, rest), NN))
    for start in range(0, tokens, TILE):
        stop = start + TILE
        query_grad = dot(kt_ref[:, :stop], ds_ref[:stop, start:stop], NN)
        put(0, start, query_grad.T * SCALE)


def unpack_kernel(recv_ref, dq_ref, dk_ref, dv_ref, sems):
    rows = dq_ref.shape[0]
    outs = (dq_ref, dk_ref, dv_ref)
    for place, ref in enumerate(outs):
        for head in range(recv_ref.shape[0]):
            pltpu.make_async_copy(
                recv_ref.at[head, place * rows : (place + 1) * rows, :],
                ref.at[:, head * HD : (head + 1) * HD],
                sems.at[place],
            ).start()
    for place, ref in enumerate(outs):
        pltpu.make_async_copy(ref, ref, sems.at[place]).wait()


def bf16(*shape):
    return jax.ShapeDtypeStruct(shape, jnp.bfloat16)


def pack(operands, count, stats=()):
    rows, width = operands[0].shape
    shape = bf16(width // HD, count * rows + bool(stats) * STATS, HD)
    scratch = [pltpu.VMEM(operand.shape, operand.dtype) for operand in operands]
    scratch += [
        pltpu.VMEM(shape.shape, shape.dtype),
        pltpu.SemaphoreType.DMA((len(operands),)),
        pltpu.SemaphoreType.DMA((count + bool(stats),)),
    ]
    with jax.named_scope("pack"):
        return pl.pallas_call(
            functools.partial(pack_kernel, count, stats),
            out_shape=shape,
            in_specs=[IN_HBM] * len(operands),
            out_specs=IN_HBM,
            scratch_shapes=scratch,
            compiler_params=pltpu.CompilerParams(vmem_limit_bytes=PACK_LIMIT),
        )(*operands)


def exchange(chunks):
    with jax.named_scope("exchange"):
        return lax.all_to_all(chunks, "ctx", 0, 0, tiled=True)


def head_grads(layout, received, rows):
    tokens = received[0].shape[0] * rows
    with jax.named_scope("head_grads"):
        return pl.pallas_call(
            functools.partial(head_kernel, layout, len(received)),
            out_shape=bf16(received[0].shape[0], 3 * rows, HD),
            in_specs=[IN_VMEM] * len(received),
            out_specs=IN_VMEM,
            scratch_shapes=(
                pltpu.VMEM((tokens, tokens), jnp.bfloat16),
                pltpu.VMEM((tokens, tokens), jnp.bfloat16),
                pltpu.VMEM((HD, tokens), jnp.bfloat16),
                pltpu.VMEM((8, tokens), jnp.float32),
                pltpu.VMEM((8, tokens), jnp.float32),
            ),
            compiler_params=pltpu.CompilerParams(vmem_limit_bytes=HEAD_LIMIT),
        )(*received)


def unpack(received, rows, width):
    with jax.named_scope("unpack"):
        return pl.pallas_call(
            unpack_kernel,
            out_shape=(bf16(rows, width),) * 3,
            in_specs=[IN_VMEM],
            out_specs=(IN_HBM,) * 3,
            scratch_shapes=(pltpu.SemaphoreType.DMA((3,)),),
            compiler_params=pltpu.CompilerParams(vmem_limit_bytes=HEAD_LIMIT),
        )(received)


def local(queries, keys, values, outputs, out_grad, log_norm):
    rows, width = queries.shape

    def at_once():
        everything = (queries, keys, values, out_grad, outputs, log_norm)
        received = exchange(pack(everything, 4, (3, 4, 5)))
        layout = {"q": (0, 0), "k": (0, rows), "v": (0, 2 * rows), "g": (0, 3 * rows), "stats": (0, 4 * rows)}
        return head_grads(layout, (received,), rows)

    def in_two():
        first = exchange(pack((out_grad, outputs, log_norm), 0, (0, 1, 2)))
        second = exchange(pack((queries, keys, values, out_grad), 4))
        layout = {"q": (1, 0), "k": (1, rows), "v": (1, 2 * rows), "g": (1, 3 * rows), "stats": (0, 0)}
        return head_grads(layout, (first, second), rows)

    grads = lax.cond(lax.axis_index("doc") % 2 == 0, in_two, at_once)
    return unpack(exchange(grads), rows, width)


def solution(mesh):
    tokens = P(("doc", "ctx"), None)
    in_specs = (tokens,) * 5 + (P(None, ("doc", "ctx")),)
    return jax.shard_map(
        local, mesh=mesh, in_specs=in_specs, out_specs=(tokens,) * 3, check_vma=False
    )
```

time: 77.7 us -> 68.4 us (0.88)
  blocking collectives: 62.2 us -> 41 us
  starting transfers between devices: 0 us -> 7.97 us
  local copies, waits for them, and re-layouts: 5.89 us -> 0 us
  waiting for transfers between devices: 0 us -> 5.7 us
  Pallas kernels: 8.51 us -> 12.3 us
    all_to_all x2, blocking collectives: 62.2 us -> 41 us  [exchange(): return lax.all_to_all(chunks, 'ctx', 0, 0, tiled=True)]
    all_to_all x0 -> x1, starting transfers between devices: none -> 7.97 us  [exchange(): return lax.all_to_all(chunks, 'ctx', 0, 0, tiled=True)]
    unnamed x12 -> x0, local copies, waits for them, and re-layouts: 5.89 us -> none
    all_to_all x0 -> x1, waiting for transfers between devices: none -> 5.7 us  [exchange(): return lax.all_to_all(chunks, 'ctx', 0, 0, tiled=True)]
    pallas_call x3 -> x4, Pallas kernels: 8.51 us -> 12.3 us  [the longest x1 6.03 us: head_grads(): pl.pallas_call(functools.partial(head_kernel, layout, len(received)), out...]
  transfers between devices with their start and end apart: 0 -> 1, of which waited for: 0 -> 1; matrix products, arithmetic and copies ran while one was open for 0% -> 0% of each run, Pallas kernels for 0% -> 4%
where the time goes in v3:
time: 68.4 us; the launch traced here: 68.1 us
  blocking collectives  41 us (60%)
  Pallas kernels  12.3 us (18%)
  starting transfers between devices  7.97 us (12%)
  waiting for transfers between devices  5.7 us (8%)
  between operations  0.83 us (1%)
    all_to_all x2, blocking collectives, exchange(): return lax.all_to_all(chunks, 'ctx', 0, 0, tiled=True)  41 us
    all_to_all x1, starting transfers between devices, exchange(): return lax.all_to_all(chunks, 'ctx', 0, 0, tiled=True)  7.97 us
    pallas_call x1, Pallas kernels, head_grads(): pl.pallas_call(functools.partial(head_kernel, layout, len(received)), out...  6.03 us
    all_to_all x1, waiting for transfers between devices, exchange(): return lax.all_to_all(chunks, 'ctx', 0, 0, tiled=True)  5.7 us
    pallas_call x2, Pallas kernels, pack(): pl.pallas_call(functools.partial(pack_kernel, count, stats), out_shape=sh...  5.09 us
  transfers between devices with their start and end apart: 1, of which 1 were waited for; matrix products, arithmetic and copies ran while one was open for 0% of the time, Pallas kernels for 4%

profile of v3, /device:TPU:0, one launch (start us, length us, event | category | flops | bytes accessed | tf_op | source)
XLA Modules:
  0.0 68.1 jit_solution(16498396487890348562)
XLA Ops:
  0.6 47.4 %conditional.1 = (bf16[16,384,128]{2,1,0:T(8,128)(2,1)S(1)}) conditional(s32[]{:T(128)} %convert_element_type.3, (bf16[128,2048]{1,0:T(8,128)(2,1)}, bf16[128,2048]{1,0:T(8,128)(2,1)}, bf16[128,2048]{1,0:T(8,128)(2,1)}, bf16[128,2048]{1,0:T(8,128)(2,1)}, bf16[128,2048]{1,0:T(8,128)(2,1)}, /*index=5*/bf16[16,128]{1,0:T(8,128)(2,1)}) %tuple.13, ...), branch_computations={%region_0.1_spmd, %region_1.2_spmd} | conditional | bytes 4390952 | solution.py:221
  0.7 2.5 %pack.4 = bf16[16,16,128]{2,1,0:T(8,128)(2,1)} custom-call(bf16[128,2048]{1,0:T(8,128)(2,1)} %get-tuple-element.33.refs_0_.refs_3_, bf16[128,2048]{1,0:T(8,128)(2,1)} %get-tuple-element.34.refs_1_, bf16[16,128]{1,0:T(8,128)(2,1)} %get-tuple-element.35.refs_2_), custom_call_target="tpu_custom_call" | custom-call | tf_op jit(solution)/shard_map/cond/branch_1_fun/pack/pallas_call | solution.py:160
  3.2 8.0 %all-to-all-start.1 = ((bf16[16,16,128]{2,1,0:T(8,128)(2,1)}), bf16[16,16,128]{2,1,0:T(8,128)(2,1)S(1)}, u32[]{:S(2)}, u32[]{:S(2)}) async-start(bf16[16,16,128]{2,1,0:T(8,128)(2,1)} %pack.4), calls=%async_computation.1 | async-start | bytes 131072 | tf_op jit(solution)/shard_map/cond/branch_1_fun/exchange/all_to_all | solution.py:172
  11.2 2.6 %pack.5 = bf16[16,512,128]{2,1,0:T(8,128)(2,1)} custom-call(bf16[128,2048]{1,0:T(8,128)(2,1)} %get-tuple-element.36.refs_0_, bf16[128,2048]{1,0:T(8,128)(2,1)} %get-tuple-element.37.refs_1_, bf16[128,2048]{1,0:T(8,128)(2,1)} %get-tuple-element.38.refs_2_, bf16[128,2048]{1,0:T(8,128)(2,1)} %get-tuple-element.33.refs_0_.refs_3_), custom_call_target="tpu_custom_call" | custom-call | tf_op jit(solution)/shard_map/cond/branch_1_fun/pack/pallas_call | solution.py:160
  13.8 5.7 %all-to-all-done.1.refs_0_ = bf16[16,16,128]{2,1,0:T(8,128)(2,1)S(1)} async-done(((bf16[16,16,128]{2,1,0:T(8,128)(2,1)}), bf16[16,16,128]{2,1,0:T(8,128)(2,1)S(1)}, u32[]{:S(2)}, u32[]{:S(2)}) %all-to-all-start.1) | async-done | bytes 65568 | tf_op jit(solution)/shard_map/cond/branch_1_fun/exchange/all_to_all | solution.py:172
  19.5 22.4 %all_to_all.18.refs_1_ = bf16[16,512,128]{2,1,0:T(8,128)(2,1)S(1)} all-to-all(bf16[16,512,128]{2,1,0:T(8,128)(2,1)} %pack.5), channel_id=1, replica_groups=mesh['ctx'=16,'doc'=8] {'ctx'}, dimensions={0} | all-to-all | bytes 4194304 | tf_op jit(solution)/shard_map/cond/branch_1_fun/exchange/all_to_all | solution.py:172
  41.8 6.0 %head_grads.3 = bf16[16,384,128]{2,1,0:T(8,128)(2,1)S(1)} custom-call(bf16[16,16,128]{2,1,0:T(8,128)(2,1)S(1)} %all-to-all-done.1.refs_0_, bf16[16,512,128]{2,1,0:T(8,128)(2,1)S(1)} %all_to_all.18.refs_1_), custom_call_target="tpu_custom_call" | custom-call | tf_op jit(solution)/shard_map/cond/branch_1_fun/head_grads/pallas_call | solution.py:178
  48.1 18.7 %all_to_all.19.recv_ref = bf16[16,384,128]{2,1,0:T(8,128)(2,1)S(1)} all-to-all(bf16[16,384,128]{2,1,0:T(8,128)(2,1)S(1)} %get-tuple-element.42), channel_id=1, replica_groups=mesh['ctx'=16,'doc'=8] {'ctx'}, dimensions={0} | all-to-all | bytes 3145728 | tf_op jit(solution)/shard_map/exchange/all_to_all | solution.py:172
  66.8 1.1 %unpack.1 = (bf16[128,2048]{1,0:T(8,128)(2,1)}, bf16[128,2048]{1,0:T(8,128)(2,1)}, bf16[128,2048]{1,0:T(8,128)(2,1)}) custom-call(bf16[16,384,128]{2,1,0:T(8,128)(2,1)S(1)} %all_to_all.19.recv_ref), custom_call_target="tpu_custom_call" | custom-call | tf_op jit(solution)/shard_map/unpack/pallas_call | solution.py:196
Async XLA Ops:
  3.2 16.2 %all-to-all-start.1 = ((bf16[16,16,128]{2,1,0:T(8,128)(2,1)}), bf16[16,16,128]{2,1,0:T(8,128)(2,1)S(1)}, u32[]{:S(2)}, u32[]{:S(2)}) async-start(bf16[16,16,128]{2,1,0:T(8,128)(2,1)} %pack.4), calls=%async_computation.1 | async-start | bytes 131072 | tf_op jit(solution)/shard_map/cond/branch_1_fun/exchange/all_to_all | solution.py:172

commit v4 on v1

v4 whole, which is shorter than its diff:
```python
import functools
import math

import jax
import jax.numpy as jnp
from jax import lax
from jax.experimental import pallas as pl
from jax.experimental.pallas import tpu as pltpu
from jax.sharding import PartitionSpec as P

HD = 128
SCALE = HD**-0.5
LOG2E = math.log2(math.e)
STATS = 16
KERNEL_LIMIT = 32 * 1024 * 1024

NT = (((1,), (1,)), ((), ()))
NN = (((1,), (0,)), ((), ()))
TN = (((0,), (0,)), ((), ()))

IN_HBM = pl.BlockSpec(memory_space=pltpu.HBM)
IN_VMEM = pl.BlockSpec(memory_space=pltpu.VMEM)


def dot(left, right, dims):
    return lax.dot_general(left, right, dims, preferred_element_type=jnp.float32)


def row_stats(grads, outs, lse):
    product = (grads.astype(jnp.float32) * outs.astype(jnp.float32)).T
    delta = jnp.sum(product, axis=0, keepdims=True)
    delta_high = delta.astype(jnp.bfloat16).astype(jnp.float32)
    which = lax.broadcasted_iota(jnp.int32, (STATS, delta.shape[1]), 0)
    stats = jnp.where(which == 1, delta_high, delta - delta_high)
    return jnp.where(which == 0, lse.astype(jnp.float32), stats).astype(jnp.bfloat16)


def score_grads(scores, dprobs, stats):
    probs = jnp.exp2(scores * (SCALE * LOG2E) - stats[0:1] * LOG2E)
    return probs, dprobs - stats[1:2] - stats[2:3]


def fetch(sources, held, sems):
    copies = [
        pltpu.make_async_copy(source, buffer, sems.at[place])
        for place, (source, buffer) in enumerate(zip(sources, held, strict=True))
    ]
    for copy in copies:
        copy.start()
    return copies


def pack_kernel(*refs):
    sources, send_ref, held, sems = refs[:6], refs[6], refs[7:13], refs[13]
    heads = send_ref.shape[0]
    rows = sources[0].shape[0]
    copies = fetch(sources, held, sems)
    for place in range(4):
        copies[place].wait()
        for head in range(heads):
            cols = slice(head * HD, (head + 1) * HD)
            send_ref[head, place * rows : (place + 1) * rows, :] = held[place][:, cols]
    copies[4].wait()
    copies[5].wait()
    for head in range(heads):
        cols = slice(head * HD, (head + 1) * HD)
        send_ref[head, 4 * rows :, :] = row_stats(
            held[3][:, cols], held[4][:, cols], held[5][head : head + 1, :]
        )


def repack_kernel(*refs):
    sources, stats_ref, send_ref, held, sems = refs[:4], refs[4], refs[5], refs[6:10], refs[10]
    heads = send_ref.shape[0]
    rows = sources[0].shape[0]
    copies = fetch(sources, held, sems)
    send_ref[:, 4 * rows :, :] = stats_ref[...]
    for place in range(4):
        copies[place].wait()
        for head in range(heads):
            cols = slice(head * HD, (head + 1) * HD)
            send_ref[head, place * rows : (place + 1) * rows, :] = held[place][:, cols]


def near_head(query, keys, values, grads, stats):
    scores = dot(keys, query, NT)
    dprobs = dot(values, grads, NT)
    probs, centred = score_grads(scores, dprobs, stats.astype(jnp.float32))
    key_pos = lax.broadcasted_iota(jnp.int32, probs.shape, 0)
    query_pos = lax.broadcasted_iota(jnp.int32, probs.shape, 1)
    probs = jnp.where(key_pos <= query_pos, probs, 0.0)
    dscores = (probs * centred).astype(jnp.bfloat16)
    query_grad = dot(dscores, keys, TN) * SCALE
    key_grad = dot(dscores, query, NN) * SCALE
    return query_grad, key_grad, dot(probs.astype(jnp.bfloat16), grads, NN)


def near_kernel(*refs):
    sources, outs, stats_ref, held, sems = refs[:6], refs[6:9], refs[9], refs[10:16], refs[16]
    for copy in fetch(sources, held, sems):
        copy.wait()
    for head in range(stats_ref.shape[0]):
        cols = slice(head * HD, (head + 1) * HD)
        parts = [held[place][:, cols] for place in range(4)]
        stats = row_stats(parts[3], held[4][:, cols], held[5][head : head + 1, :])
        stats_ref[head] = stats
        for ref, term in zip(outs, near_head(*parts, stats), strict=True):
            ref[:, cols] = term


class Head:
    def __init__(self, x_ref, out_ref, p_ref, ds_ref, kt_ref, stats_ref):
        self.x, self.out, self.p, self.ds, self.kt, self.stats = x_ref, out_ref, p_ref, ds_ref, kt_ref, stats_ref
        self.rows = out_ref.shape[1] // 3
        self.tokens = x_ref.shape[0] * self.rows
        for start in range(0, self.tokens, self.rows):
            cols = slice(start, start + self.rows)
            stats = x_ref[start // self.rows, 4 * self.rows :, :].astype(jnp.float32)
            stats_ref[0:1, cols] = stats[0:1] * LOG2E
            stats_ref[1:2, cols] = stats[1:2] + stats[2:3]
            kt_ref[:, cols] = self.piece(1, start, self.rows).T

    def piece(self, place, start, count):
        rows = self.rows
        blocks = slice(start // rows, (start + count) // rows)
        return self.x[blocks, place * rows : (place + 1) * rows, :].reshape(count, HD)

    def put(self, place, start, value):
        rows = self.rows
        for step in range(value.shape[0] // rows):
            part = value[step * rows : (step + 1) * rows].astype(jnp.bfloat16)
            self.out[start // rows + step, place * rows : (place + 1) * rows, :] = part

    def tile(self, keys, values, key_start, start, count, masked=False):
        key_rows, cols = slice(key_start, key_start + keys.shape[0]), slice(start, start + count)
        scores = dot(keys, self.piece(0, start, count), NT)
        dprobs = dot(values, self.piece(3, start, count), NT)
        probs = jnp.exp2(scores * (SCALE * LOG2E) - self.stats[0:1, cols])
        if masked:
            key_pos = lax.broadcasted_iota(jnp.int32, probs.shape, 0)
            query_pos = lax.broadcasted_iota(jnp.int32, probs.shape, 1)
            probs = jnp.where(key_pos <= query_pos, probs, 0.0)
        dscores = probs * (dprobs - self.stats[1:2, cols])
        self.p[key_rows, cols] = probs.astype(jnp.bfloat16)
        self.ds[key_rows, cols] = dscores.astype(jnp.bfloat16)


def whole_head_kernel(*refs):
    head = Head(*refs)
    step, tokens = 2 * head.rows, head.tokens
    for first in range(0, tokens, step):
        keys, values = head.piece(1, first, step), head.piece(2, first, step)
        for start in range(first, tokens, step):
            head.tile(keys, values, first, start, step, masked=start == first)
        rest, part = tokens - first, slice(first, first + step)
        head.put(1, first, dot(head.ds[part, first:], head.piece(0, first, rest), NN) * SCALE)
        head.put(2, first, dot(head.p[part, first:], head.piece(3, first, rest), NN))
    for first in range(0, tokens, step):
        stop = first + step
        head.put(0, first, dot(head.kt[:, :stop], head.ds[:stop, first:stop], NN).T * SCALE)


def far_head_kernel(*refs):
    head = Head(*refs)
    rows, tokens = head.rows, head.tokens
    step = 2 * rows
    for first in range(0, tokens, step):
        second, stop = first + rows, first + step
        keys, values = head.piece(1, first, step), head.piece(2, first, step)
        head.tile(keys[:rows], values[:rows], first, second, rows)
        for start in range(stop, tokens, step):
            head.tile(keys, values, first, start, step)
        for place, source, factor, ref in ((1, 0, SCALE, head.ds), (2, 3, 1.0, head.p)):
            total = dot(ref[first:second, second:stop], head.piece(source, second, rows), NN)
            after = jnp.zeros_like(total)
            if stop < tokens:
                far = dot(ref[first:stop, stop:], head.piece(source, stop, tokens - stop), NN)
                total, after = total + far[:rows], far[rows:]
            head.put(place, first, total * factor)
            head.put(place, second, after * factor)
    for first in range(0, tokens, step):
        second, stop = first + rows, first + step
        total = dot(head.kt[:, first:second], head.ds[first:second, second:stop], NN)
        before = jnp.zeros_like(total)
        if first > 0:
            far = dot(head.kt[:, :first], head.ds[:first, first:stop], NN)
            before, total = far[:, :rows], total + far[:, rows:]
        head.put(0, first, before.T * SCALE)
        head.put(0, second, total.T * SCALE)


def unpack_kernel(recv_ref, *refs):
    outs, sems = refs[:3], refs[3]
    rows = outs[0].shape[0]
    for place, ref in enumerate(outs):
        for head in range(recv_ref.shape[0]):
            pltpu.make_async_copy(
                recv_ref.at[head, place * rows : (place + 1) * rows, :],
                ref.at[:, head * HD : (head + 1) * HD],
                sems.at[place],
            ).start()
    for place, ref in enumerate(outs):
        pltpu.make_async_copy(ref, ref, sems.at[place]).wait()


def unpack_add_kernel(recv_ref, *refs):
    near, outs, sums, sems = refs[:3], refs[3:6], refs[6:9], refs[9]
    rows = outs[0].shape[0]
    copies = []
    for place, (part, buffer, ref) in enumerate(zip(near, sums, outs, strict=True)):
        for head in range(recv_ref.shape[0]):
            cols = slice(head * HD, (head + 1) * HD)
            far = recv_ref[head, place * rows : (place + 1) * rows, :].astype(jnp.float32)
            buffer[:, cols] = (far + part[:, cols]).astype(jnp.bfloat16)
        copies.append(pltpu.make_async_copy(buffer, ref, sems.at[place]))
        copies[-1].start()
    for copy in copies:
        copy.wait()


def bf16(*shape):
    return jax.ShapeDtypeStruct(shape, jnp.bfloat16)


def f32(*shape):
    return jax.ShapeDtypeStruct(shape, jnp.float32)


def call(kernel, name, in_specs, out_specs, out_shape, scratch):
    def run(*operands):
        operands = [
            pltpu.with_memory_space_constraint(operand, pltpu.HBM) if spec is IN_HBM else operand
            for spec, operand in zip(in_specs, operands, strict=True)
        ]
        with jax.named_scope(name):
            return pl.pallas_call(
                kernel,
                out_shape=out_shape,
                in_specs=in_specs,
                out_specs=out_specs,
                scratch_shapes=scratch,
                compiler_params=pltpu.CompilerParams(vmem_limit_bytes=KERNEL_LIMIT),
            )(*operands)

    return run


def exchange(chunks):
    with jax.named_scope("exchange"):
        return lax.all_to_all(chunks, "ctx", 0, 0, tiled=True)


def local(*arguments):
    queries, keys, values, outputs, out_grad, log_norm = arguments
    rows, width = queries.shape
    heads = width // HD
    tokens = rows * lax.axis_size("ctx")
    everything = (queries, keys, values, out_grad, outputs, log_norm)
    held = [pltpu.VMEM(operand.shape, operand.dtype) for operand in everything]
    chunk = bf16(heads, 4 * rows + STATS, HD)
    result = (bf16(rows, width),) * 3
    copies = pltpu.SemaphoreType.DMA

    def head_grads(kernel, x):
        scratch = (
            pltpu.VMEM((tokens, tokens), jnp.bfloat16),
            pltpu.VMEM((tokens, tokens), jnp.bfloat16),
            pltpu.VMEM((HD, tokens), jnp.bfloat16),
            pltpu.VMEM((8, tokens), jnp.float32),
        )
        shape = bf16(heads, 3 * rows, HD)
        return call(kernel, "head_grads", [IN_VMEM], IN_VMEM, shape, scratch)(x)

    def goes_first():
        pack = call(pack_kernel, "pack", [IN_HBM] * 6, IN_VMEM, chunk, (*held, copies((6,))))
        back = exchange(head_grads(whole_head_kernel, exchange(pack(*everything))))
        unpack = call(unpack_kernel, "unpack", [IN_VMEM], (IN_HBM,) * 3, result, (copies((3,)),))
        return unpack(back)

    def goes_second():
        shapes = (*(f32(rows, width),) * 3, bf16(heads, STATS, HD))
        near = call(near_kernel, "near", [IN_HBM] * 6, (IN_VMEM,) * 4, shapes, (*held, copies((6,))))
        *terms, stats = near(*everything)
        specs, scratch = [IN_HBM] * 4 + [IN_VMEM], (*held[:4], copies((4,)))
        pack = call(repack_kernel, "pack", specs, IN_VMEM, chunk, scratch)
        back = exchange(head_grads(far_head_kernel, exchange(pack(*everything[:4], stats))))
        scratch = (*(pltpu.VMEM((rows, width), jnp.bfloat16),) * 3, copies((3,)))
        unpack = call(unpack_add_kernel, "unpack", [IN_VMEM] * 4, (IN_HBM,) * 3, result, scratch)
        return unpack(back, *terms)

    return lax.cond(lax.axis_index("doc") % 2 == 1, goes_first, goes_second)


def solution(mesh):
    tokens = P(("doc", "ctx"), None)
    in_specs = (tokens,) * 5 + (P(None, ("doc", "ctx")),)
    return jax.shard_map(
        local, mesh=mesh, in_specs=in_specs, out_specs=(tokens,) * 3, check_vma=False
    )
```

time: 77.7 us -> 67.4 us (0.87)
  blocking collectives: 62.2 us -> 51.8 us
  local copies, waits for them, and re-layouts: 5.89 us -> 0 us
  Pallas kernels: 8.51 us -> 14.3 us
    all_to_all x2, blocking collectives: 62.2 us -> 51.8 us  [exchange(): return lax.all_to_all(chunks, 'ctx', 0, 0, tiled=True)]
    unnamed x12 -> x0, local copies, waits for them, and re-layouts: 5.89 us -> none
    pallas_call x3 -> x4, Pallas kernels: 8.51 us -> 14.3 us  [run(): pl.pallas_call(kernel, out_shape=out_shape, in_specs=in_specs, out_specs=...]
where the time goes in v4:
time: 67.4 us; the launch traced here: 67.2 us
  blocking collectives  51.8 us (77%)
  Pallas kernels  14.3 us (21%)
  between operations  0.82 us (1%)
    all_to_all x2, blocking collectives, exchange(): return lax.all_to_all(chunks, 'ctx', 0, 0, tiled=True)  51.8 us
    pallas_call x4, Pallas kernels, run(): pl.pallas_call(kernel, out_shape=out_shape, in_specs=in_specs, out_specs=...  14.3 us

profile of v4, /device:TPU:0, one launch (start us, length us, event | category | flops | bytes accessed | tf_op | source)
XLA Modules:
  0.0 67.2 jit_solution(16222849972497595535)
XLA Ops:
  0.6 66.4 %conditional.1 = ((bf16[128,2048]{1,0:T(8,128)(2,1)}, bf16[128,2048]{1,0:T(8,128)(2,1)}, bf16[128,2048]{1,0:T(8,128)(2,1)})) conditional(s32[]{:T(128)} %convert_element_type.3, (bf16[128,2048]{1,0:T(8,128)(2,1)}, bf16[128,2048]{1,0:T(8,128)(2,1)}, bf16[128,2048]{1,0:T(8,128)(2,1)}, bf16[128,2048]{1,0:T(8,128)(2,1)}, bf16[128,2048]{1,0:T(8,128)(2,1)}, ...), branch_computations={%region_0.1_spmd, %region_1.2_spmd} | conditional | bytes 7471112 | solution.py:291
  0.7 5.6 %near.1 = (f32[128,2048]{1,0:T(8,128)S(1)}, f32[128,2048]{1,0:T(8,128)S(1)}, f32[128,2048]{1,0:T(8,128)S(1)}, bf16[16,16,128]{2,1,0:T(8,128)(2,1)S(1)}) custom-call(bf16[128,2048]{1,0:T(8,128)(2,1)} %get-tuple-element.24.refs_0_, bf16[128,2048]{1,0:T(8,128)(2,1)} %get-tuple-element.25.refs_1_, bf16[128,2048]{1,0:T(8,128)(2,1)} %get-tuple-element.26.refs_2_, ...), custom_call_target="tpu_custom_call" | custom-call | tf_op jit(solution)/shard_map/cond/branch_0_fun/near/pallas_call | solution.py:236
  6.3 1.6 %pack.2 = bf16[16,528,128]{2,1,0:T(8,128)(2,1)S(1)} custom-call(bf16[128,2048]{1,0:T(8,128)(2,1)} %get-tuple-element.24.refs_0_, bf16[128,2048]{1,0:T(8,128)(2,1)} %get-tuple-element.25.refs_1_, bf16[128,2048]{1,0:T(8,128)(2,1)} %get-tuple-element.26.refs_2_, bf16[128,2048]{1,0:T(8,128)(2,1)} %get-tuple-element.27.refs_3_, ...), custom_call_target="tpu_custom_call" | custom-call | tf_op jit(solution)/shard_map/cond/branch_0_fun/pack/pallas_call | solution.py:236
  7.9 31.8 %all_to_all.16.refs_0_ = bf16[16,528,128]{2,1,0:T(8,128)(2,1)S(1)} all-to-all(bf16[16,528,128]{2,1,0:T(8,128)(2,1)S(1)} %pack.2), channel_id=1, replica_groups=mesh['ctx'=16,'doc'=8] {'ctx'}, dimensions={0} | all-to-all | bytes 4325376 | tf_op jit(solution)/shard_map/cond/branch_0_fun/exchange/all_to_all | solution.py:250
  39.8 5.7 %head_grads.2 = bf16[16,384,128]{2,1,0:T(8,128)(2,1)S(1)} custom-call(bf16[16,528,128]{2,1,0:T(8,128)(2,1)S(1)} %all_to_all.16.refs_0_), custom_call_target="tpu_custom_call" | custom-call | tf_op jit(solution)/shard_map/cond/branch_0_fun/head_grads/pallas_call | solution.py:236
  45.5 20.0 %all_to_all.17.recv_ref = bf16[16,384,128]{2,1,0:T(8,128)(2,1)S(1)} all-to-all(bf16[16,384,128]{2,1,0:T(8,128)(2,1)S(1)} %head_grads.2), channel_id=1, replica_groups=mesh['ctx'=16,'doc'=8] {'ctx'}, dimensions={0} | all-to-all | bytes 3145728 | tf_op jit(solution)/shard_map/cond/branch_0_fun/exchange/all_to_all | solution.py:250
  65.5 1.3 %unpack.2 = (bf16[128,2048]{1,0:T(8,128)(2,1)}, bf16[128,2048]{1,0:T(8,128)(2,1)}, bf16[128,2048]{1,0:T(8,128)(2,1)}) custom-call(bf16[16,384,128]{2,1,0:T(8,128)(2,1)S(1)} %all_to_all.17.recv_ref, f32[128,2048]{1,0:T(8,128)S(1)} %get-tuple-element.31.refs_0_, f32[128,2048]{1,0:T(8,128)S(1)} %get-tuple-element.32.refs_1_, ...), custom_call_target="tpu_custom_call" | custom-call | tf_op jit(solution)/shard_map/cond/branch_0_fun/unpack/pallas_call | solution.py:236

commit v5 on v4

--- a/solution.py
+++ b/solution.py
@@ -40,13 +40,13 @@
     return probs, dprobs - stats[1:2] - stats[2:3]
 
 
-def fetch(sources, held, sems):
+def fetch(sources, held, sems, order):
     copies = [
         pltpu.make_async_copy(source, buffer, sems.at[place])
         for place, (source, buffer) in enumerate(zip(sources, held, strict=True))
     ]
-    for copy in copies:
-        copy.start()
+    for place in order:
+        copies[place].start()
     return copies
 
 
@@ -54,28 +54,17 @@
     sources, send_ref, held, sems = refs[:6], refs[6], refs[7:13], refs[13]
     heads = send_ref.shape[0]
     rows = sources[0].shape[0]
-    copies = fetch(sources, held, sems)
-    for place in range(4):
+    copies = fetch(sources, held, sems, (5, 4, 3, 0, 1, 2))
+    for place in (5, 4, 3):
         copies[place].wait()
-        for head in range(heads):
-            cols = slice(head * HD, (head + 1) * HD)
-            send_ref[head, place * rows : (place + 1) * rows, :] = held[place][:, cols]
-    copies[4].wait()
-    copies[5].wait()
     for head in range(heads):
         cols = slice(head * HD, (head + 1) * HD)
+        grads = held[3][:, cols]
+        send_ref[head, 3 * rows : 4 * rows, :] = grads
         send_ref[head, 4 * rows :, :] = row_stats(
-            held[3][:, cols], held[4][:, cols], held[5][head : head + 1, :]
+            grads, held[4][:, cols], held[5][head : head + 1, :]
         )
-
-
-def repack_kernel(*refs):
-    sources, stats_ref, send_ref, held, sems = refs[:4], refs[4], refs[5], refs[6:10], refs[10]
-    heads = send_ref.shape[0]
-    rows = sources[0].shape[0]
-    copies = fetch(sources, held, sems)
-    send_ref[:, 4 * rows :, :] = stats_ref[...]
-    for place in range(4):
+    for place in range(3):
         copies[place].wait()
         for head in range(heads):
             cols = slice(head * HD, (head + 1) * HD)
@@ -97,7 +86,7 @@
 
 def near_kernel(*refs):
     sources, outs, stats_ref, held, sems = refs[:6], refs[6:9], refs[9], refs[10:16], refs[16]
-    for copy in fetch(sources, held, sems):
+    for copy in fetch(sources, held, sems, range(6)):
         copy.wait()
     for head in range(stats_ref.shape[0]):
         cols = slice(head * HD, (head + 1) * HD)
@@ -281,9 +270,10 @@
         shapes = (*(f32(rows, width),) * 3, bf16(heads, STATS, HD))
         near = call(near_kernel, "near", [IN_HBM] * 6, (IN_VMEM,) * 4, shapes, (*held, copies((6,))))
         *terms, stats = near(*everything)
-        specs, scratch = [IN_HBM] * 4 + [IN_VMEM], (*held[:4], copies((4,)))
-        pack = call(repack_kernel, "pack", specs, IN_VMEM, chunk, scratch)
-        back = exchange(head_grads(far_head_kernel, exchange(pack(*everything[:4], stats))))
+        with jax.named_scope("pack"):
+            by_heads = [x.reshape(rows, heads, HD).transpose(1, 0, 2) for x in everything[:4]]
+            send = jnp.concatenate((*by_heads, stats), axis=1)
+        back = exchange(head_grads(far_head_kernel, exchange(send)))
         scratch = (*(pltpu.VMEM((rows, width), jnp.bfloat16),) * 3, copies((3,)))
         unpack = call(unpack_add_kernel, "unpack", [IN_VMEM] * 4, (IN_HBM,) * 3, result, scratch)
         return unpack(back, *terms)

time: 67.4 us -> 66.3 us (0.984)
  local copies, waits for them, and re-layouts: 0 us -> 3.62 us
  blocking collectives: 51.8 us -> 48.6 us
  Pallas kernels: 14.3 us -> 12.7 us
    all_to_all x2, blocking collectives: 51.8 us -> 48.6 us  [exchange(): return lax.all_to_all(chunks, 'ctx', 0, 0, tiled=True)]
    another operation x0 -> x4, local copies, waits for them, and re-layouts: none -> 2.2 us
    pallas_call x4 -> x3, Pallas kernels: 14.3 us -> 12.7 us  [run(): pl.pallas_call(kernel, out_shape=out_shape, in_specs=in_specs, out_specs=...]
    reshape x0 -> x4, local copies, waits for them, and re-layouts: none -> 1.14 us  [goes_second(): x.reshape(rows, heads, HD).transpose(1, 0, 2)]
where the time goes in v5:
time: 66.3 us; the launch traced here: 66.1 us
  blocking collectives  48.6 us (73%)
  Pallas kernels  12.7 us (19%)
  local copies, waits for them, and re-layouts  3.62 us (5%)
  between operations  0.82 us (1%)
    all_to_all x2, blocking collectives, exchange(): return lax.all_to_all(chunks, 'ctx', 0, 0, tiled=True)  48.6 us
    pallas_call x3, Pallas kernels, run(): pl.pallas_call(kernel, out_shape=out_shape, in_specs=in_specs, out_specs=...  12.7 us
    another operation x4, local copies, waits for them, and re-layouts  2.2 us

profile of v5, /device:TPU:0, one launch (start us, length us, event | category | flops | bytes accessed | tf_op | source)
XLA Modules:
  0.0 66.1 jit_solution(1730283987649639392)
XLA Ops:
  0.6 65.3 %conditional.1 = ((bf16[128,2048]{1,0:T(8,128)(2,1)}, bf16[128,2048]{1,0:T(8,128)(2,1)}, bf16[128,2048]{1,0:T(8,128)(2,1)})) conditional(s32[]{:T(128)} %convert_element_type.3, (bf16[128,2048]{1,0:T(8,128)(2,1)}, bf16[128,2048]{1,0:T(8,128)(2,1)}, bf16[128,2048]{1,0:T(8,128)(2,1)}, bf16[128,2048]{1,0:T(8,128)(2,1)}, bf16[128,2048]{1,0:T(8,128)(2,1)}, ...), branch_computations={%region_0.1_spmd, %region_1.2_spmd} | conditional | bytes 26476636 | solution.py:281
  0.7 0.0 copy-start
  0.7 0.0 copy-start.1
  0.7 1.4 %copy.15 = bf16[128,2048]{0,1:T(8,128)(2,1)S(1)} copy(bf16[128,2048]{1,0:T(8,128)(2,1)} %get-tuple-element.24.refs_0_) | data formatting | bytes 1048576 | tf_op jit(solution)/shard_map
  2.1 0.3 copy.16
  2.4 0.0 copy-start.2
  2.4 0.0 copy-done
  2.4 0.3 copy.17
  2.7 0.3 copy.18
  3.0 0.0 copy-done.1
  3.0 0.3 copy.19
  3.2 0.3 copy.20
  3.5 0.0 copy-done.2
  3.5 0.3 copy.21
  3.8 0.3 copy.22
  4.2 0.1 bitcast_dynamic-update-slice_fusion.2
  4.2 0.1 bitcast_dynamic-update-slice_fusion.1
  4.3 0.1 bitcast_dynamic-update-slice_fusion
  4.4 5.6 %near.1 = (f32[128,2048]{1,0:T(8,128)S(1)}, f32[128,2048]{1,0:T(8,128)S(1)}, f32[128,2048]{1,0:T(8,128)S(1)}, bf16[16,16,128]{2,1,0:T(8,128)(2,1)S(1)}) custom-call(bf16[128,2048]{1,0:T(8,128)(2,1)} %get-tuple-element.24.refs_0_, bf16[128,2048]{1,0:T(8,128)(2,1)} %get-tuple-element.25.refs_1_, bf16[128,2048]{1,0:T(8,128)(2,1)} %get-tuple-element.26.refs_2_, ...), custom_call_target="tpu_custom_call" | custom-call | tf_op jit(solution)/shard_map/cond/branch_0_fun/near/pallas_call | solution.py:225
  10.0 29.7 %all_to_all.16.refs_0_ = bf16[16,528,128]{2,1,0:T(8,128)(2,1)S(1)} all-to-all(bf16[16,528,128]{2,1,0:T(8,128)(2,1)S(1)} %constant_dynamic-update-slice_fusion), channel_id=1, replica_groups=mesh['ctx'=16,'doc'=8] {'ctx'}, dimensions={0} | all-to-all | bytes 4325376 | tf_op jit(solution)/shard_map/cond/branch_0_fun/exchange/all_to_all | solution.py:239
  39.7 5.7 %head_grads.2 = bf16[16,384,128]{2,1,0:T(8,128)(2,1)S(1)} custom-call(bf16[16,528,128]{2,1,0:T(8,128)(2,1)S(1)} %all_to_all.16.refs_0_), custom_call_target="tpu_custom_call" | custom-call | tf_op jit(solution)/shard_map/cond/branch_0_fun/head_grads/pallas_call | solution.py:225
  45.4 19.0 %all_to_all.17.recv_ref = bf16[16,384,128]{2,1,0:T(8,128)(2,1)S(1)} all-to-all(bf16[16,384,128]{2,1,0:T(8,128)(2,1)S(1)} %head_grads.2), channel_id=1, replica_groups=mesh['ctx'=16,'doc'=8] {'ctx'}, dimensions={0} | all-to-all | bytes 3145728 | tf_op jit(solution)/shard_map/cond/branch_0_fun/exchange/all_to_all | solution.py:239
  64.4 1.3 %unpack.2 = (bf16[128,2048]{1,0:T(8,128)(2,1)}, bf16[128,2048]{1,0:T(8,128)(2,1)}, bf16[128,2048]{1,0:T(8,128)(2,1)}) custom-call(bf16[16,384,128]{2,1,0:T(8,128)(2,1)S(1)} %all_to_all.17.recv_ref, f32[128,2048]{1,0:T(8,128)S(1)} %get-tuple-element.31.refs_0_, f32[128,2048]{1,0:T(8,128)S(1)} %get-tuple-element.32.refs_1_, ...), custom_call_target="tpu_custom_call" | custom-call | tf_op jit(solution)/shard_map/cond/branch_0_fun/unpack/pallas_call | solution.py:225
  (2 shorter events, 0.0 us)
Async XLA Ops:
  0.7 1.7 %copy-start = (bf16[128,2048]{1,0:T(8,128)(2,1)S(1)}, bf16[128,2048]{1,0:T(8,128)(2,1)}, u32[]{:S(2)}) copy-start(bf16[128,2048]{1,0:T(8,128)(2,1)} %get-tuple-element.25.refs_1_) | copy-start | bytes 1572868 | tf_op jit(solution)/shard_map/cond
  0.7 2.3 %copy-start.1 = (bf16[128,2048]{1,0:T(8,128)(2,1)S(1)}, bf16[128,2048]{1,0:T(8,128)(2,1)}, u32[]{:S(2)}) copy-start(bf16[128,2048]{1,0:T(8,128)(2,1)} %get-tuple-element.26.refs_2_) | copy-start | bytes 1572868 | tf_op jit(solution)/shard_map/cond
  2.4 1.2 %copy-start.2 = (bf16[128,2048]{1,0:T(8,128)(2,1)S(1)}, bf16[128,2048]{1,0:T(8,128)(2,1)}, u32[]{:S(2)}) copy-start(bf16[128,2048]{1,0:T(8,128)(2,1)} %get-tuple-element.27.refs_3_) | copy-start | bytes 1572868 | tf_op jit(solution)/shard_map/cond

commit v6 on v5

--- a/solution.py
+++ b/solution.py
@@ -98,16 +98,18 @@
 
 
 class Head:
-    def __init__(self, x_ref, out_ref, p_ref, ds_ref, kt_ref, stats_ref):
-        self.x, self.out, self.p, self.ds, self.kt, self.stats = x_ref, out_ref, p_ref, ds_ref, kt_ref, stats_ref
+    def __init__(self, x_ref, out_ref, p_ref, ds_ref, qt_ref, gt_ref, lse_ref, delta_ref):
+        self.x, self.out, self.p, self.ds, self.qt, self.gt = x_ref, out_ref, p_ref, ds_ref, qt_ref, gt_ref
+        self.lse, self.delta = lse_ref, delta_ref
         self.rows = out_ref.shape[1] // 3
         self.tokens = x_ref.shape[0] * self.rows
         for start in range(0, self.tokens, self.rows):
-            cols = slice(start, start + self.rows)
+            part = slice(start, start + self.rows)
             stats = x_ref[start // self.rows, 4 * self.rows :, :].astype(jnp.float32)
-            stats_ref[0:1, cols] = stats[0:1] * LOG2E
-            stats_ref[1:2, cols] = stats[1:2] + stats[2:3]
-            kt_ref[:, cols] = self.piece(1, start, self.rows).T
+            for ref, row in ((lse_ref, stats[0:1] * LOG2E), (delta_ref, stats[1:2] + stats[2:3])):
+                ref[part, :] = jnp.broadcast_to(row, (HD, self.rows)).T
+            qt_ref[:, part] = self.piece(0, start, self.rows).T
+            gt_ref[:, part] = self.piece(3, start, self.rows).T
 
     def piece(self, place, start, count):
         rows = self.rows
@@ -120,33 +122,35 @@
             part = value[step * rows : (step + 1) * rows].astype(jnp.bfloat16)
             self.out[start // rows + step, place * rows : (place + 1) * rows, :] = part
 
-    def tile(self, keys, values, key_start, start, count, masked=False):
-        key_rows, cols = slice(key_start, key_start + keys.shape[0]), slice(start, start + count)
-        scores = dot(keys, self.piece(0, start, count), NT)
-        dprobs = dot(values, self.piece(3, start, count), NT)
-        probs = jnp.exp2(scores * (SCALE * LOG2E) - self.stats[0:1, cols])
+    def tile(self, query, grads, start, key_start, count, masked=False):
+        part, cols = slice(start, start + query.shape[0]), slice(key_start, key_start + count)
+        scores = dot(query, self.piece(1, key_start, count), NT)
+        dprobs = dot(grads, self.piece(2, key_start, count), NT)
+        lse = jnp.concatenate([self.lse[part, :]] * (count // HD), axis=1)
+        delta = jnp.concatenate([self.delta[part, :]] * (count // HD), axis=1)
+        probs = jnp.exp2(scores * (SCALE * LOG2E) - lse)
         if masked:
-            key_pos = lax.broadcasted_iota(jnp.int32, probs.shape, 0)
-            query_pos = lax.broadcasted_iota(jnp.int32, probs.shape, 1)
+            query_pos = lax.broadcasted_iota(jnp.int32, probs.shape, 0)
+            key_pos = lax.broadcasted_iota(jnp.int32, probs.shape, 1)
             probs = jnp.where(key_pos <= query_pos, probs, 0.0)
-        dscores = probs * (dprobs - self.stats[1:2, cols])
-        self.p[key_rows, cols] = probs.astype(jnp.bfloat16)
-        self.ds[key_rows, cols] = dscores.astype(jnp.bfloat16)
+        dscores = probs * (dprobs - delta)
+        self.p[part, cols] = probs.astype(jnp.bfloat16)
+        self.ds[part, cols] = dscores.astype(jnp.bfloat16)
 
 
 def whole_head_kernel(*refs):
     head = Head(*refs)
     step, tokens = 2 * head.rows, head.tokens
     for first in range(0, tokens, step):
-        keys, values = head.piece(1, first, step), head.piece(2, first, step)
-        for start in range(first, tokens, step):
-            head.tile(keys, values, first, start, step, masked=start == first)
-        rest, part = tokens - first, slice(first, first + step)
-        head.put(1, first, dot(head.ds[part, first:], head.piece(0, first, rest), NN) * SCALE)
-        head.put(2, first, dot(head.p[part, first:], head.piece(3, first, rest), NN))
-    for first in range(0, tokens, step):
         stop = first + step
-        head.put(0, first, dot(head.kt[:, :stop], head.ds[:stop, first:stop], NN).T * SCALE)
+        query, grads = head.piece(0, first, step), head.piece(3, first, step)
+        for start in range(0, stop, step):
+            head.tile(query, grads, first, start, step, masked=start == first)
+        head.put(0, first, dot(head.ds[first:stop, :stop], head.piece(1, 0, stop), NN) * SCALE)
+    for first in range(0, tokens, step):
+        cols = slice(first, first + step)
+        head.put(1, first, dot(head.qt[:, first:], head.ds[first:, cols], NN).T * SCALE)
+        head.put(2, first, dot(head.gt[:, first:], head.p[first:, cols], NN).T)
 
 
 def far_head_kernel(*refs):
@@ -155,27 +159,27 @@
     step = 2 * rows
     for first in range(0, tokens, step):
         second, stop = first + rows, first + step
-        keys, values = head.piece(1, first, step), head.piece(2, first, step)
-        head.tile(keys[:rows], values[:rows], first, second, rows)
-        for start in range(stop, tokens, step):
-            head.tile(keys, values, first, start, step)
-        for place, source, factor, ref in ((1, 0, SCALE, head.ds), (2, 3, 1.0, head.p)):
-            total = dot(ref[first:second, second:stop], head.piece(source, second, rows), NN)
+        query, grads = head.piece(0, first, step), head.piece(3, first, step)
+        for start in range(0, first, step):
+            head.tile(query, grads, first, start, step)
+        head.tile(query[rows:], grads[rows:], second, first, rows)
+        total = dot(head.ds[second:stop, first:second], head.piece(1, first, rows), NN)
+        before = jnp.zeros_like(total)
+        if first > 0:
+            far = dot(head.ds[first:stop, :first], head.piece(1, 0, first), NN)
+            before, total = far[:rows], total + far[rows:]
+        head.put(0, first, before * SCALE)
+        head.put(0, second, total * SCALE)
+    for first in range(0, tokens, step):
+        second, stop = first + rows, first + step
+        for place, ref, turned, factor in ((1, head.ds, head.qt, SCALE), (2, head.p, head.gt, 1.0)):
+            total = dot(turned[:, second:stop], ref[second:stop, first:second], NN)
             after = jnp.zeros_like(total)
             if stop < tokens:
-                far = dot(ref[first:stop, stop:], head.piece(source, stop, tokens - stop), NN)
-                total, after = total + far[:rows], far[rows:]
-            head.put(place, first, total * factor)
-            head.put(place, second, after * factor)
-    for first in range(0, tokens, step):
-        second, stop = first + rows, first + step
-        total = dot(head.kt[:, first:second], head.ds[first:second, second:stop], NN)
-        before = jnp.zeros_like(total)
-        if first > 0:
-            far = dot(head.kt[:, :first], head.ds[:first, first:stop], NN)
-            before, total = far[:, :rows], total + far[:, rows:]
-        head.put(0, first, before.T * SCALE)
-        head.put(0, second, total.T * SCALE)
+                far = dot(turned[:, stop:], ref[stop:, first:stop], NN)
+                total, after = total + far[:, :rows], far[:, rows:]
+            head.put(place, first, total.T * factor)
+            head.put(place, second, after.T * factor)
 
 
 def unpack_kernel(recv_ref, *refs):
@@ -255,7 +259,9 @@
             pltpu.VMEM((tokens, tokens), jnp.bfloat16),
             pltpu.VMEM((tokens, tokens), jnp.bfloat16),
             pltpu.VMEM((HD, tokens), jnp.bfloat16),
-            pltpu.VMEM((8, tokens), jnp.float32),
+            pltpu.VMEM((HD, tokens), jnp.bfloat16),
+            pltpu.VMEM((tokens, HD), jnp.float32),
+            pltpu.VMEM((tokens, HD), jnp.float32),
         )
         shape = bf16(heads, 3 * rows, HD)
         return call(kernel, "head_grads", [IN_VMEM], IN_VMEM, shape, scratch)(x)

time: 66.3 us -> 65.8 us (level)
  no operation moved by 1% of the time
where the time goes in v6:
time: 65.8 us; the launch traced here: 65.6 us
  blocking collectives  48.6 us (74%)
  Pallas kernels  12.1 us (18%)
  local copies, waits for them, and re-layouts  3.62 us (6%)
  between operations  0.82 us (1%)
    all_to_all x2, blocking collectives, exchange(): return lax.all_to_all(chunks, 'ctx', 0, 0, tiled=True)  48.6 us
    pallas_call x3, Pallas kernels, run(): pl.pallas_call(kernel, out_shape=out_shape, in_specs=in_specs, out_specs=...  12.1 us
    another operation x4, local copies, waits for them, and re-layouts  2.2 us

profile of v6, /device:TPU:0, one launch (start us, length us, event | category | flops | bytes accessed | tf_op | source)
XLA Modules:
  0.0 65.6 jit_solution(13138463611726727823)
XLA Ops:
  0.6 64.8 %conditional.1 = ((bf16[128,2048]{1,0:T(8,128)(2,1)}, bf16[128,2048]{1,0:T(8,128)(2,1)}, bf16[128,2048]{1,0:T(8,128)(2,1)})) conditional(s32[]{:T(128)} %convert_element_type.3, (bf16[128,2048]{1,0:T(8,128)(2,1)}, bf16[128,2048]{1,0:T(8,128)(2,1)}, bf16[128,2048]{1,0:T(8,128)(2,1)}, bf16[128,2048]{1,0:T(8,128)(2,1)}, bf16[128,2048]{1,0:T(8,128)(2,1)}, ...), branch_computations={%region_0.1_spmd, %region_1.2_spmd} | conditional | bytes 26476636 | solution.py:287
  0.7 0.0 copy-start
  0.7 0.0 copy-start.1
  0.7 1.4 %copy.15 = bf16[128,2048]{0,1:T(8,128)(2,1)S(1)} copy(bf16[128,2048]{1,0:T(8,128)(2,1)} %get-tuple-element.24.refs_0_) | data formatting | bytes 1048576 | tf_op jit(solution)/shard_map
  2.1 0.3 copy.16
  2.4 0.0 copy-start.2
  2.4 0.0 copy-done
  2.4 0.3 copy.17
  2.7 0.3 copy.18
  3.0 0.0 copy-done.1
  3.0 0.3 copy.19
  3.2 0.3 copy.20
  3.5 0.0 copy-done.2
  3.5 0.3 copy.21
  3.8 0.3 copy.22
  4.2 0.1 bitcast_dynamic-update-slice_fusion.2
  4.2 0.1 bitcast_dynamic-update-slice_fusion.1
  4.3 0.1 bitcast_dynamic-update-slice_fusion
  4.4 5.6 %near.1 = (f32[128,2048]{1,0:T(8,128)S(1)}, f32[128,2048]{1,0:T(8,128)S(1)}, f32[128,2048]{1,0:T(8,128)S(1)}, bf16[16,16,128]{2,1,0:T(8,128)(2,1)S(1)}) custom-call(bf16[128,2048]{1,0:T(8,128)(2,1)} %get-tuple-element.24.refs_0_, bf16[128,2048]{1,0:T(8,128)(2,1)} %get-tuple-element.25.refs_1_, bf16[128,2048]{1,0:T(8,128)(2,1)} %get-tuple-element.26.refs_2_, ...), custom_call_target="tpu_custom_call" | custom-call | tf_op jit(solution)/shard_map/cond/branch_0_fun/near/pallas_call | solution.py:229
  10.0 29.7 %all_to_all.16.refs_0_ = bf16[16,528,128]{2,1,0:T(8,128)(2,1)S(1)} all-to-all(bf16[16,528,128]{2,1,0:T(8,128)(2,1)S(1)} %constant_dynamic-update-slice_fusion), channel_id=1, replica_groups=mesh['ctx'=16,'doc'=8] {'ctx'}, dimensions={0} | all-to-all | bytes 4325376 | tf_op jit(solution)/shard_map/cond/branch_0_fun/exchange/all_to_all | solution.py:243
  39.7 5.2 %head_grads.2 = bf16[16,384,128]{2,1,0:T(8,128)(2,1)S(1)} custom-call(bf16[16,528,128]{2,1,0:T(8,128)(2,1)S(1)} %all_to_all.16.refs_0_), custom_call_target="tpu_custom_call" | custom-call | tf_op jit(solution)/shard_map/cond/branch_0_fun/head_grads/pallas_call | solution.py:229
  44.9 19.0 %all_to_all.17.recv_ref = bf16[16,384,128]{2,1,0:T(8,128)(2,1)S(1)} all-to-all(bf16[16,384,128]{2,1,0:T(8,128)(2,1)S(1)} %head_grads.2), channel_id=1, replica_groups=mesh['ctx'=16,'doc'=8] {'ctx'}, dimensions={0} | all-to-all | bytes 3145728 | tf_op jit(solution)/shard_map/cond/branch_0_fun/exchange/all_to_all | solution.py:243
  63.9 1.3 %unpack.2 = (bf16[128,2048]{1,0:T(8,128)(2,1)}, bf16[128,2048]{1,0:T(8,128)(2,1)}, bf16[128,2048]{1,0:T(8,128)(2,1)}) custom-call(bf16[16,384,128]{2,1,0:T(8,128)(2,1)S(1)} %all_to_all.17.recv_ref, f32[128,2048]{1,0:T(8,128)S(1)} %get-tuple-element.31.refs_0_, f32[128,2048]{1,0:T(8,128)S(1)} %get-tuple-element.32.refs_1_, ...), custom_call_target="tpu_custom_call" | custom-call | tf_op jit(solution)/shard_map/cond/branch_0_fun/unpack/pallas_call | solution.py:229
  (2 shorter events, 0.0 us)
Async XLA Ops:
  0.7 1.7 %copy-start = (bf16[128,2048]{1,0:T(8,128)(2,1)S(1)}, bf16[128,2048]{1,0:T(8,128)(2,1)}, u32[]{:S(2)}) copy-start(bf16[128,2048]{1,0:T(8,128)(2,1)} %get-tuple-element.25.refs_1_) | copy-start | bytes 1572868 | tf_op jit(solution)/shard_map/cond
  0.7 2.3 %copy-start.1 = (bf16[128,2048]{1,0:T(8,128)(2,1)S(1)}, bf16[128,2048]{1,0:T(8,128)(2,1)}, u32[]{:S(2)}) copy-start(bf16[128,2048]{1,0:T(8,128)(2,1)} %get-tuple-element.26.refs_2_) | copy-start | bytes 1572868 | tf_op jit(solution)/shard_map/cond
  2.4 1.2 %copy-start.2 = (bf16[128,2048]{1,0:T(8,128)(2,1)S(1)}, bf16[128,2048]{1,0:T(8,128)(2,1)}, u32[]{:S(2)}) copy-start(bf16[128,2048]{1,0:T(8,128)(2,1)} %get-tuple-element.27.refs_3_) | copy-start | bytes 1572868 | tf_op jit(solution)/shard_map/cond

commit v7 on v6

--- a/solution.py
+++ b/solution.py
@@ -138,31 +138,47 @@
         self.ds[part, cols] = dscores.astype(jnp.bfloat16)
 
 
+def last_to_first(tokens, step, tiles, sums):
+    done = None
+    for first in reversed(range(0, tokens, step)):
+        tiles(first)
+        if done is not None:
+            sums(done)
+        done = first
+    sums(done)
+
+
 def whole_head_kernel(*refs):
     head = Head(*refs)
-    step, tokens = 2 * head.rows, head.tokens
-    for first in range(0, tokens, step):
+    step = 2 * head.rows
+
+    def tiles(first):
+        query, grads = head.piece(0, first, step), head.piece(3, first, step)
+        for start in range(0, first + step, step):
+            head.tile(query, grads, first, start, step, masked=start == first)
+
+    def sums(first):
         stop = first + step
-        query, grads = head.piece(0, first, step), head.piece(3, first, step)
-        for start in range(0, stop, step):
-            head.tile(query, grads, first, start, step, masked=start == first)
         head.put(0, first, dot(head.ds[first:stop, :stop], head.piece(1, 0, stop), NN) * SCALE)
-    for first in range(0, tokens, step):
-        cols = slice(first, first + step)
-        head.put(1, first, dot(head.qt[:, first:], head.ds[first:, cols], NN).T * SCALE)
-        head.put(2, first, dot(head.gt[:, first:], head.p[first:, cols], NN).T)
+        head.put(1, first, dot(head.qt[:, first:], head.ds[first:, first:stop], NN).T * SCALE)
+        head.put(2, first, dot(head.gt[:, first:], head.p[first:, first:stop], NN).T)
+
+    last_to_first(head.tokens, step, tiles, sums)
 
 
 def far_head_kernel(*refs):
     head = Head(*refs)
     rows, tokens = head.rows, head.tokens
     step = 2 * rows
-    for first in range(0, tokens, step):
-        second, stop = first + rows, first + step
+
+    def tiles(first):
         query, grads = head.piece(0, first, step), head.piece(3, first, step)
         for start in range(0, first, step):
             head.tile(query, grads, first, start, step)
-        head.tile(query[rows:], grads[rows:], second, first, rows)
+        head.tile(query[rows:], grads[rows:], first + rows, first, rows)
+
+    def sums(first):
+        second, stop = first + rows, first + step
         total = dot(head.ds[second:stop, first:second], head.piece(1, first, rows), NN)
         before = jnp.zeros_like(total)
         if first > 0:
@@ -170,8 +186,6 @@
             before, total = far[:rows], total + far[rows:]
         head.put(0, first, before * SCALE)
         head.put(0, second, total * SCALE)
-    for first in range(0, tokens, step):
-        second, stop = first + rows, first + step
         for place, ref, turned, factor in ((1, head.ds, head.qt, SCALE), (2, head.p, head.gt, 1.0)):
             total = dot(turned[:, second:stop], ref[second:stop, first:second], NN)
             after = jnp.zeros_like(total)
@@ -180,6 +194,8 @@
                 total, after = total + far[:, :rows], far[:, rows:]
             head.put(place, first, total.T * factor)
             head.put(place, second, after.T * factor)
+
+    last_to_first(tokens, step, tiles, sums)
 
 
 def unpack_kernel(recv_ref, *refs):

time: 65.8 us -> 65.4 us (level)
  no operation moved by 1% of the time
where the time goes in v7:
time: 65.4 us; the launch traced here: 65.2 us
  blocking collectives  48.6 us (74%)
  Pallas kernels  11.7 us (18%)
  local copies, waits for them, and re-layouts  3.62 us (6%)
  between operations  0.82 us (1%)
    all_to_all x2, blocking collectives, exchange(): return lax.all_to_all(chunks, 'ctx', 0, 0, tiled=True)  48.6 us
    pallas_call x3, Pallas kernels, run(): pl.pallas_call(kernel, out_shape=out_shape, in_specs=in_specs, out_specs=...  11.7 us
    another operation x4, local copies, waits for them, and re-layouts  2.2 us

profile of v7, /device:TPU:0, one launch (start us, length us, event | category | flops | bytes accessed | tf_op | source)
XLA Modules:
  0.0 65.2 jit_solution(18284762084125804997)
XLA Ops:
  0.6 64.4 %conditional.1 = ((bf16[128,2048]{1,0:T(8,128)(2,1)}, bf16[128,2048]{1,0:T(8,128)(2,1)}, bf16[128,2048]{1,0:T(8,128)(2,1)})) conditional(s32[]{:T(128)} %convert_element_type.3, (bf16[128,2048]{1,0:T(8,128)(2,1)}, bf16[128,2048]{1,0:T(8,128)(2,1)}, bf16[128,2048]{1,0:T(8,128)(2,1)}, bf16[128,2048]{1,0:T(8,128)(2,1)}, bf16[128,2048]{1,0:T(8,128)(2,1)}, ...), branch_computations={%region_0.1_spmd, %region_1.2_spmd} | conditional | bytes 26476636 | solution.py:303
  0.7 0.0 copy-start
  0.7 0.0 copy-start.1
  0.7 1.4 %copy.15 = bf16[128,2048]{0,1:T(8,128)(2,1)S(1)} copy(bf16[128,2048]{1,0:T(8,128)(2,1)} %get-tuple-element.24.refs_0_) | data formatting | bytes 1048576 | tf_op jit(solution)/shard_map
  2.1 0.3 copy.16
  2.4 0.0 copy-start.2
  2.4 0.0 copy-done
  2.4 0.3 copy.17
  2.7 0.3 copy.18
  3.0 0.0 copy-done.1
  3.0 0.3 copy.19
  3.2 0.3 copy.20
  3.5 0.0 copy-done.2
  3.5 0.3 copy.21
  3.8 0.3 copy.22
  4.2 0.1 bitcast_dynamic-update-slice_fusion.2
  4.2 0.1 bitcast_dynamic-update-slice_fusion.1
  4.3 0.1 bitcast_dynamic-update-slice_fusion
  4.4 5.6 %near.1 = (f32[128,2048]{1,0:T(8,128)S(1)}, f32[128,2048]{1,0:T(8,128)S(1)}, f32[128,2048]{1,0:T(8,128)S(1)}, bf16[16,16,128]{2,1,0:T(8,128)(2,1)S(1)}) custom-call(bf16[128,2048]{1,0:T(8,128)(2,1)} %get-tuple-element.24.refs_0_, bf16[128,2048]{1,0:T(8,128)(2,1)} %get-tuple-element.25.refs_1_, bf16[128,2048]{1,0:T(8,128)(2,1)} %get-tuple-element.26.refs_2_, ...), custom_call_target="tpu_custom_call" | custom-call | tf_op jit(solution)/shard_map/cond/branch_0_fun/near/pallas_call | solution.py:245
  10.0 29.7 %all_to_all.16.refs_0_ = bf16[16,528,128]{2,1,0:T(8,128)(2,1)S(1)} all-to-all(bf16[16,528,128]{2,1,0:T(8,128)(2,1)S(1)} %constant_dynamic-update-slice_fusion), channel_id=1, replica_groups=mesh['ctx'=16,'doc'=8] {'ctx'}, dimensions={0} | all-to-all | bytes 4325376 | tf_op jit(solution)/shard_map/cond/branch_0_fun/exchange/all_to_all | solution.py:259
  39.7 4.8 %head_grads.2 = bf16[16,384,128]{2,1,0:T(8,128)(2,1)S(1)} custom-call(bf16[16,528,128]{2,1,0:T(8,128)(2,1)S(1)} %all_to_all.16.refs_0_), custom_call_target="tpu_custom_call" | custom-call | tf_op jit(solution)/shard_map/cond/branch_0_fun/head_grads/pallas_call | solution.py:245
  44.5 19.0 %all_to_all.17.recv_ref = bf16[16,384,128]{2,1,0:T(8,128)(2,1)S(1)} all-to-all(bf16[16,384,128]{2,1,0:T(8,128)(2,1)S(1)} %head_grads.2), channel_id=1, replica_groups=mesh['ctx'=16,'doc'=8] {'ctx'}, dimensions={0} | all-to-all | bytes 3145728 | tf_op jit(solution)/shard_map/cond/branch_0_fun/exchange/all_to_all | solution.py:259
  63.5 1.3 %unpack.2 = (bf16[128,2048]{1,0:T(8,128)(2,1)}, bf16[128,2048]{1,0:T(8,128)(2,1)}, bf16[128,2048]{1,0:T(8,128)(2,1)}) custom-call(bf16[16,384,128]{2,1,0:T(8,128)(2,1)S(1)} %all_to_all.17.recv_ref, f32[128,2048]{1,0:T(8,128)S(1)} %get-tuple-element.31.refs_0_, f32[128,2048]{1,0:T(8,128)S(1)} %get-tuple-element.32.refs_1_, ...), custom_call_target="tpu_custom_call" | custom-call | tf_op jit(solution)/shard_map/cond/branch_0_fun/unpack/pallas_call | solution.py:245
  (2 shorter events, 0.1 us)
Async XLA Ops:
  0.7 1.7 %copy-start = (bf16[128,2048]{1,0:T(8,128)(2,1)S(1)}, bf16[128,2048]{1,0:T(8,128)(2,1)}, u32[]{:S(2)}) copy-start(bf16[128,2048]{1,0:T(8,128)(2,1)} %get-tuple-element.25.refs_1_) | copy-start | bytes 1572868 | tf_op jit(solution)/shard_map/cond
  0.7 2.3 %copy-start.1 = (bf16[128,2048]{1,0:T(8,128)(2,1)S(1)}, bf16[128,2048]{1,0:T(8,128)(2,1)}, u32[]{:S(2)}) copy-start(bf16[128,2048]{1,0:T(8,128)(2,1)} %get-tuple-element.26.refs_2_) | copy-start | bytes 1572868 | tf_op jit(solution)/shard_map/cond
  2.4 1.2 %copy-start.2 = (bf16[128,2048]{1,0:T(8,128)(2,1)S(1)}, bf16[128,2048]{1,0:T(8,128)(2,1)}, u32[]{:S(2)}) copy-start(bf16[128,2048]{1,0:T(8,128)(2,1)} %get-tuple-element.27.refs_3_) | copy-start | bytes 1572868 | tf_op jit(solution)/shard_map/cond

commit v8 on v7

--- a/solution.py
+++ b/solution.py
@@ -11,7 +11,7 @@
 HD = 128
 SCALE = HD**-0.5
 LOG2E = math.log2(math.e)
-STATS = 16
+GROUP = 8
 KERNEL_LIMIT = 32 * 1024 * 1024
 
 NT = (((1,), (1,)), ((), ()))
@@ -30,7 +30,7 @@
     product = (grads.astype(jnp.float32) * outs.astype(jnp.float32)).T
     delta = jnp.sum(product, axis=0, keepdims=True)
     delta_high = delta.astype(jnp.bfloat16).astype(jnp.float32)
-    which = lax.broadcasted_iota(jnp.int32, (STATS, delta.shape[1]), 0)
+    which = lax.broadcasted_iota(jnp.int32, (GROUP, delta.shape[1]), 0)
     stats = jnp.where(which == 1, delta_high, delta - delta_high)
     return jnp.where(which == 0, lse.astype(jnp.float32), stats).astype(jnp.bfloat16)
 
@@ -38,6 +38,11 @@
 def score_grads(scores, dprobs, stats):
     probs = jnp.exp2(scores * (SCALE * LOG2E) - stats[0:1] * LOG2E)
     return probs, dprobs - stats[1:2] - stats[2:3]
+
+
+def put_rows(send_ref, head, place, value):
+    count = value.shape[0] // GROUP
+    send_ref[head, place * count : (place + 1) * count] = value.reshape(count, GROUP, HD)
 
 
 def fetch(sources, held, sems, order):
@@ -60,15 +65,15 @@
     for head in range(heads):
         cols = slice(head * HD, (head + 1) * HD)
         grads = held[3][:, cols]
-        send_ref[head, 3 * rows : 4 * rows, :] = grads
-        send_ref[head, 4 * rows :, :] = row_stats(
+        put_rows(send_ref, head, 3, grads)
+        send_ref[head, 4 * rows // GROUP] = row_stats(
             grads, held[4][:, cols], held[5][head : head + 1, :]
         )
     for place in range(3):
         copies[place].wait()
         for head in range(heads):
             cols = slice(head * HD, (head + 1) * HD)
-            send_ref[head, place * rows : (place + 1) * rows, :] = held[place][:, cols]
+            put_rows(send_ref, head, place, held[place][:, cols])
 
 
 def near_head(query, keys, values, grads, stats):
@@ -105,16 +110,16 @@
         self.tokens = x_ref.shape[0] * self.rows
         for start in range(0, self.tokens, self.rows):
             part = slice(start, start + self.rows)
-            stats = x_ref[start // self.rows, 4 * self.rows :, :].astype(jnp.float32)
+            stats = x_ref[start // self.rows, 4 * self.rows // GROUP].astype(jnp.float32)
             for ref, row in ((lse_ref, stats[0:1] * LOG2E), (delta_ref, stats[1:2] + stats[2:3])):
                 ref[part, :] = jnp.broadcast_to(row, (HD, self.rows)).T
             qt_ref[:, part] = self.piece(0, start, self.rows).T
             gt_ref[:, part] = self.piece(3, start, self.rows).T
 
     def piece(self, place, start, count):
-        rows = self.rows
-        blocks = slice(start // rows, (start + count) // rows)
-        return self.x[blocks, place * rows : (place + 1) * rows, :].reshape(count, HD)
+        blocks = slice(start // self.rows, (start + count) // self.rows)
+        groups = self.rows // GROUP
+        return self.x[blocks, place * groups : (place + 1) * groups].reshape(count, HD)
 
     def put(self, place, start, value):
         rows = self.rows
@@ -266,7 +271,7 @@
     tokens = rows * lax.axis_size("ctx")
     everything = (queries, keys, values, out_grad, outputs, log_norm)
     held = [pltpu.VMEM(operand.shape, operand.dtype) for operand in everything]
-    chunk = bf16(heads, 4 * rows + STATS, HD)
+    chunk = bf16(heads, 4 * rows // GROUP + 1, GROUP, HD)
     result = (bf16(rows, width),) * 3
     copies = pltpu.SemaphoreType.DMA
 
@@ -289,12 +294,12 @@
         return unpack(back)
 
     def goes_second():
-        shapes = (*(f32(rows, width),) * 3, bf16(heads, STATS, HD))
+        shapes = (*(f32(rows, width),) * 3, bf16(heads, GROUP, HD))
         near = call(near_kernel, "near", [IN_HBM] * 6, (IN_VMEM,) * 4, shapes, (*held, copies((6,))))
         *terms, stats = near(*everything)
         with jax.named_scope("pack"):
             by_heads = [x.reshape(rows, heads, HD).transpose(1, 0, 2) for x in everything[:4]]
-            send = jnp.concatenate((*by_heads, stats), axis=1)
+            send = jnp.concatenate((*by_heads, stats), axis=1).reshape(chunk.shape)
         back = exchange(head_grads(far_head_kernel, exchange(send)))
         scratch = (*(pltpu.VMEM((rows, width), jnp.bfloat16),) * 3, copies((3,)))
         unpack = call(unpack_add_kernel, "unpack", [IN_VMEM] * 4, (IN_HBM,) * 3, result, scratch)

time: 65.4 us -> 65.1 us (level)
  local copies, waits for them, and re-layouts: 3.62 us -> 2.79 us
    cond x10 -> x8, local copies, waits for them, and re-layouts: 0.26 us -> 2.78 us
    another operation x4 -> x0, local copies, waits for them, and re-layouts: 2.2 us -> none
    reshape x4 -> x0, local copies, waits for them, and re-layouts: 1.14 us -> none  [goes_second(): x.reshape(rows, heads, HD).transpose(1, 0, 2)]
where the time goes in v8:
time: 65.1 us; the launch traced here: 64.8 us
  blocking collectives  49.2 us (76%)
  Pallas kernels  11.7 us (18%)
  local copies, waits for them, and re-layouts  2.79 us (4%)
  between operations  0.82 us (1%)
    all_to_all x2, blocking collectives, exchange(): return lax.all_to_all(chunks, 'ctx', 0, 0, tiled=True)  49.2 us
    pallas_call x3, Pallas kernels, run(): pl.pallas_call(kernel, out_shape=out_shape, in_specs=in_specs, out_specs=...  11.7 us
    cond x8, local copies, waits for them, and re-layouts  2.78 us

profile of v8, /device:TPU:0, one launch (start us, length us, event | category | flops | bytes accessed | tf_op | source)
XLA Modules:
  0.0 64.8 jit_solution(6520678102307767554)
XLA Ops:
  0.6 64.0 %conditional.1 = ((bf16[128,2048]{1,0:T(8,128)(2,1)}, bf16[128,2048]{1,0:T(8,128)(2,1)}, bf16[128,2048]{1,0:T(8,128)(2,1)})) conditional(s32[]{:T(128)} %convert_element_type.3, (bf16[128,2048]{1,0:T(8,128)(2,1)}, bf16[128,2048]{1,0:T(8,128)(2,1)}, bf16[128,2048]{1,0:T(8,128)(2,1)}, bf16[128,2048]{1,0:T(8,128)(2,1)}, bf16[128,2048]{1,0:T(8,128)(2,1)}, ...), branch_computations={%region_0.1_spmd, %region_1.2_spmd} | conditional | bytes 15859776 | solution.py:308
  0.7 0.0 copy-start
  0.7 0.0 copy-start.1
  0.7 1.2 %fusion.3 = bf16[16,520,128]{2,1,0:T(8,128)(2,1)S(1)} fusion(bf16[128,2048]{1,0:T(8,128)(2,1)} %get-tuple-element.24.refs_0_), kind=kLoop, calls=%fused_computation.7 | loop fusion | bytes 1048576 | tf_op jit(solution)/shard_map/cond
  1.9 1.2 %fusion.2 = bf16[16,520,128]{2,1,0:T(8,128)(2,1)S(1)} fusion(bf16[16,520,128]{2,1,0:T(8,128)(2,1)S(1)} %fusion.3, bf16[128,2048]{1,0:T(8,128)(2,1)} %get-tuple-element.25.refs_1_), kind=kLoop, calls=%fused_computation.5 | loop fusion | bytes 1048576 | tf_op jit(solution)/shard_map/cond
  3.1 0.0 copy-done
  3.1 0.2 fusion.1
  3.3 0.0 copy-done.1
  3.3 0.2 fusion
  3.5 5.6 %near.1 = (f32[128,2048]{1,0:T(8,128)S(1)}, f32[128,2048]{1,0:T(8,128)S(1)}, f32[128,2048]{1,0:T(8,128)S(1)}, bf16[16,8,128]{2,1,0:T(8,128)(2,1)S(1)}) custom-call(bf16[128,2048]{1,0:T(8,128)(2,1)} %get-tuple-element.24.refs_0_, bf16[128,2048]{1,0:T(8,128)(2,1)} %get-tuple-element.25.refs_1_, bf16[128,2048]{1,0:T(8,128)(2,1)} %get-tuple-element.26.refs_2_, ...), custom_call_target="tpu_custom_call" | custom-call | tf_op jit(solution)/shard_map/cond/branch_0_fun/near/pallas_call | solution.py:250
  9.1 30.3 %all_to_all.16.refs_0_ = bf16[16,65,8,128]{3,2,1,0:T(8,128)(2,1)S(1)} all-to-all(bf16[16,65,8,128]{3,2,1,0:T(8,128)(2,1)S(1)} %bitcast.45), channel_id=1, replica_groups=mesh['ctx'=16,'doc'=8] {'ctx'}, dimensions={0} | all-to-all | bytes 4259840 | tf_op jit(solution)/shard_map/cond/branch_0_fun/exchange/all_to_all | solution.py:264
  39.4 4.8 %head_grads.2 = bf16[16,384,128]{2,1,0:T(8,128)(2,1)S(1)} custom-call(bf16[16,65,8,128]{3,2,1,0:T(8,128)(2,1)S(1)} %all_to_all.16.refs_0_), custom_call_target="tpu_custom_call" | custom-call | tf_op jit(solution)/shard_map/cond/branch_0_fun/head_grads/pallas_call | solution.py:250
  44.2 18.9 %all_to_all.17.recv_ref = bf16[16,384,128]{2,1,0:T(8,128)(2,1)S(1)} all-to-all(bf16[16,384,128]{2,1,0:T(8,128)(2,1)S(1)} %head_grads.2), channel_id=1, replica_groups=mesh['ctx'=16,'doc'=8] {'ctx'}, dimensions={0} | all-to-all | bytes 3145728 | tf_op jit(solution)/shard_map/cond/branch_0_fun/exchange/all_to_all | solution.py:264
  63.1 1.3 %unpack.2 = (bf16[128,2048]{1,0:T(8,128)(2,1)}, bf16[128,2048]{1,0:T(8,128)(2,1)}, bf16[128,2048]{1,0:T(8,128)(2,1)}) custom-call(bf16[16,384,128]{2,1,0:T(8,128)(2,1)S(1)} %all_to_all.17.recv_ref, f32[128,2048]{1,0:T(8,128)S(1)} %get-tuple-element.31.refs_0_, f32[128,2048]{1,0:T(8,128)S(1)} %get-tuple-element.32.refs_1_, ...), custom_call_target="tpu_custom_call" | custom-call | tf_op jit(solution)/shard_map/cond/branch_0_fun/unpack/pallas_call | solution.py:250
  (1 shorter events, 0.0 us)
Async XLA Ops:
  0.7 2.5 %copy-start = (bf16[128,2048]{1,0:T(8,128)(2,1)S(1)}, bf16[128,2048]{1,0:T(8,128)(2,1)}, u32[]{:S(2)}) copy-start(bf16[128,2048]{1,0:T(8,128)(2,1)} %get-tuple-element.26.refs_2_) | copy-start | bytes 1572868 | tf_op jit(solution)/shard_map/cond
  0.7 2.6 %copy-start.1 = (bf16[128,2048]{1,0:T(8,128)(2,1)S(1)}, bf16[128,2048]{1,0:T(8,128)(2,1)}, u32[]{:S(2)}) copy-start(bf16[128,2048]{1,0:T(8,128)(2,1)} %get-tuple-element.27.refs_3_) | copy-start | bytes 1572868 | tf_op jit(solution)/shard_map/cond

commit v9 on v8

--- a/solution.py
+++ b/solution.py
@@ -58,22 +58,37 @@
 def pack_kernel(*refs):
     sources, send_ref, held, sems = refs[:6], refs[6], refs[7:13], refs[13]
     heads = send_ref.shape[0]
-    rows = sources[0].shape[0]
-    copies = fetch(sources, held, sems, (5, 4, 3, 0, 1, 2))
-    for place in (5, 4, 3):
-        copies[place].wait()
-    for head in range(heads):
-        cols = slice(head * HD, (head + 1) * HD)
-        grads = held[3][:, cols]
-        put_rows(send_ref, head, 3, grads)
-        send_ref[head, 4 * rows // GROUP] = row_stats(
-            grads, held[4][:, cols], held[5][head : head + 1, :]
-        )
+    rows, width = sources[0].shape
+    half = width // 2
+    lse = pltpu.make_async_copy(sources[5], held[5], sems.at[0])
+    lse.start()
+    copies = {}
+    for place in ((4, 3), (0,), (1,), (2,)):
+        for start in (0, half):
+            for which in place:
+                cols = slice(start, start + half)
+                copy = pltpu.make_async_copy(
+                    sources[which].at[:, cols], held[which].at[:, cols], sems.at[len(copies) + 1]
+                )
+                copy.start()
+                copies[which, start] = copy
+    lse.wait()
+    for start in (0, half):
+        copies[4, start].wait()
+        copies[3, start].wait()
+        for head in range(start // HD, (start + half) // HD):
+            cols = slice(head * HD, (head + 1) * HD)
+            grads = held[3][:, cols]
+            put_rows(send_ref, head, 3, grads)
+            send_ref[head, 4 * rows // GROUP] = row_stats(
+                grads, held[4][:, cols], held[5][head : head + 1, :]
+            )
     for place in range(3):
-        copies[place].wait()
-        for head in range(heads):
-            cols = slice(head * HD, (head + 1) * HD)
-            put_rows(send_ref, head, place, held[place][:, cols])
+        for start in (0, half):
+            copies[place, start].wait()
+            for head in range(start // HD, (start + half) // HD):
+                cols = slice(head * HD, (head + 1) * HD)
+                put_rows(send_ref, head, place, held[place][:, cols])
 
 
 def near_head(query, keys, values, grads, stats):
@@ -219,15 +234,20 @@
 
 def unpack_add_kernel(recv_ref, *refs):
     near, outs, sums, sems = refs[:3], refs[3:6], refs[6:9], refs[9]
-    rows = outs[0].shape[0]
+    rows, width = outs[0].shape
+    half = width // 2
     copies = []
     for place, (part, buffer, ref) in enumerate(zip(near, sums, outs, strict=True)):
-        for head in range(recv_ref.shape[0]):
-            cols = slice(head * HD, (head + 1) * HD)
-            far = recv_ref[head, place * rows : (place + 1) * rows, :].astype(jnp.float32)
-            buffer[:, cols] = (far + part[:, cols]).astype(jnp.bfloat16)
-        copies.append(pltpu.make_async_copy(buffer, ref, sems.at[place]))
-        copies[-1].start()
+        for start in range(0, width, half):
+            for head in range(start // HD, (start + half) // HD):
+                cols = slice(head * HD, (head + 1) * HD)
+                far = recv_ref[head, place * rows : (place + 1) * rows, :].astype(jnp.float32)
+                buffer[:, cols] = (far + part[:, cols]).astype(jnp.bfloat16)
+            cols = slice(start, start + half)
+            copies.append(
+                pltpu.make_async_copy(buffer.at[:, cols], ref.at[:, cols], sems.at[len(copies)])
+            )
+            copies[-1].start()
     for copy in copies:
         copy.wait()
 
@@ -288,7 +308,7 @@
         return call(kernel, "head_grads", [IN_VMEM], IN_VMEM, shape, scratch)(x)
 
     def goes_first():
-        pack = call(pack_kernel, "pack", [IN_HBM] * 6, IN_VMEM, chunk, (*held, copies((6,))))
+        pack = call(pack_kernel, "pack", [IN_HBM] * 6, IN_VMEM, chunk, (*held, copies((11,))))
         back = exchange(head_grads(whole_head_kernel, exchange(pack(*everything))))
         unpack = call(unpack_kernel, "unpack", [IN_VMEM], (IN_HBM,) * 3, result, (copies((3,)),))
         return unpack(back)
@@ -301,7 +321,7 @@
             by_heads = [x.reshape(rows, heads, HD).transpose(1, 0, 2) for x in everything[:4]]
             send = jnp.concatenate((*by_heads, stats), axis=1).reshape(chunk.shape)
         back = exchange(head_grads(far_head_kernel, exchange(send)))
-        scratch = (*(pltpu.VMEM((rows, width), jnp.bfloat16),) * 3, copies((3,)))
+        scratch = (*(pltpu.VMEM((rows, width), jnp.bfloat16),) * 3, copies((6,)))
         unpack = call(unpack_add_kernel, "unpack", [IN_VMEM] * 4, (IN_HBM,) * 3, result, scratch)
         return unpack(back, *terms)
 

time: 65.1 us -> 65 us (level)
  no operation moved by 1% of the time
where the time goes in v9:
time: 65 us; the launch traced here: 64.7 us
  blocking collectives  49.2 us (76%)
  Pallas kernels  11.7 us (18%)
  local copies, waits for them, and re-layouts  2.79 us (4%)
  between operations  0.82 us (1%)
    all_to_all x2, blocking collectives, exchange(): return lax.all_to_all(chunks, 'ctx', 0, 0, tiled=True)  49.2 us
    pallas_call x3, Pallas kernels, run(): pl.pallas_call(kernel, out_shape=out_shape, in_specs=in_specs, out_specs=...  11.7 us
    cond x8, local copies, waits for them, and re-layouts  2.78 us

profile of v9, /device:TPU:0, one launch (start us, length us, event | category | flops | bytes accessed | tf_op | source)
XLA Modules:
  0.0 64.7 jit_solution(992827643665969550)
XLA Ops:
  0.6 63.9 %conditional.1 = ((bf16[128,2048]{1,0:T(8,128)(2,1)}, bf16[128,2048]{1,0:T(8,128)(2,1)}, bf16[128,2048]{1,0:T(8,128)(2,1)})) conditional(s32[]{:T(128)} %convert_element_type.3, (bf16[128,2048]{1,0:T(8,128)(2,1)}, bf16[128,2048]{1,0:T(8,128)(2,1)}, bf16[128,2048]{1,0:T(8,128)(2,1)}, bf16[128,2048]{1,0:T(8,128)(2,1)}, bf16[128,2048]{1,0:T(8,128)(2,1)}, ...), branch_computations={%region_0.1_spmd, %region_1.2_spmd} | conditional | bytes 15859776 | solution.py:328
  0.7 0.0 copy-start
  0.7 0.0 copy-start.1
  0.7 1.2 %fusion.3 = bf16[16,520,128]{2,1,0:T(8,128)(2,1)S(1)} fusion(bf16[128,2048]{1,0:T(8,128)(2,1)} %get-tuple-element.24.refs_0_), kind=kLoop, calls=%fused_computation.7 | loop fusion | bytes 1048576 | tf_op jit(solution)/shard_map/cond
  1.9 1.2 %fusion.2 = bf16[16,520,128]{2,1,0:T(8,128)(2,1)S(1)} fusion(bf16[16,520,128]{2,1,0:T(8,128)(2,1)S(1)} %fusion.3, bf16[128,2048]{1,0:T(8,128)(2,1)} %get-tuple-element.25.refs_1_), kind=kLoop, calls=%fused_computation.5 | loop fusion | bytes 1048576 | tf_op jit(solution)/shard_map/cond
  3.1 0.0 copy-done
  3.1 0.2 fusion.1
  3.3 0.0 copy-done.1
  3.3 0.2 fusion
  3.5 5.6 %near.1 = (f32[128,2048]{1,0:T(8,128)S(1)}, f32[128,2048]{1,0:T(8,128)S(1)}, f32[128,2048]{1,0:T(8,128)S(1)}, bf16[16,8,128]{2,1,0:T(8,128)(2,1)S(1)}) custom-call(bf16[128,2048]{1,0:T(8,128)(2,1)} %get-tuple-element.24.refs_0_, bf16[128,2048]{1,0:T(8,128)(2,1)} %get-tuple-element.25.refs_1_, bf16[128,2048]{1,0:T(8,128)(2,1)} %get-tuple-element.26.refs_2_, ...), custom_call_target="tpu_custom_call" | custom-call | tf_op jit(solution)/shard_map/cond/branch_0_fun/near/pallas_call | solution.py:270
  9.1 30.3 %all_to_all.16.refs_0_ = bf16[16,65,8,128]{3,2,1,0:T(8,128)(2,1)S(1)} all-to-all(bf16[16,65,8,128]{3,2,1,0:T(8,128)(2,1)S(1)} %bitcast.45), channel_id=1, replica_groups=mesh['ctx'=16,'doc'=8] {'ctx'}, dimensions={0} | all-to-all | bytes 4259840 | tf_op jit(solution)/shard_map/cond/branch_0_fun/exchange/all_to_all | solution.py:284
  39.4 4.8 %head_grads.2 = bf16[16,384,128]{2,1,0:T(8,128)(2,1)S(1)} custom-call(bf16[16,65,8,128]{3,2,1,0:T(8,128)(2,1)S(1)} %all_to_all.16.refs_0_), custom_call_target="tpu_custom_call" | custom-call | tf_op jit(solution)/shard_map/cond/branch_0_fun/head_grads/pallas_call | solution.py:270
  44.2 18.9 %all_to_all.17.recv_ref = bf16[16,384,128]{2,1,0:T(8,128)(2,1)S(1)} all-to-all(bf16[16,384,128]{2,1,0:T(8,128)(2,1)S(1)} %head_grads.2), channel_id=1, replica_groups=mesh['ctx'=16,'doc'=8] {'ctx'}, dimensions={0} | all-to-all | bytes 3145728 | tf_op jit(solution)/shard_map/cond/branch_0_fun/exchange/all_to_all | solution.py:284
  63.1 1.2 %unpack.2 = (bf16[128,2048]{1,0:T(8,128)(2,1)}, bf16[128,2048]{1,0:T(8,128)(2,1)}, bf16[128,2048]{1,0:T(8,128)(2,1)}) custom-call(bf16[16,384,128]{2,1,0:T(8,128)(2,1)S(1)} %all_to_all.17.recv_ref, f32[128,2048]{1,0:T(8,128)S(1)} %get-tuple-element.31.refs_0_, f32[128,2048]{1,0:T(8,128)S(1)} %get-tuple-element.32.refs_1_, ...), custom_call_target="tpu_custom_call" | custom-call | tf_op jit(solution)/shard_map/cond/branch_0_fun/unpack/pallas_call | solution.py:270
  (1 shorter events, 0.0 us)
Async XLA Ops:
  0.7 2.5 %copy-start = (bf16[128,2048]{1,0:T(8,128)(2,1)S(1)}, bf16[128,2048]{1,0:T(8,128)(2,1)}, u32[]{:S(2)}) copy-start(bf16[128,2048]{1,0:T(8,128)(2,1)} %get-tuple-element.26.refs_2_) | copy-start | bytes 1572868 | tf_op jit(solution)/shard_map/cond
  0.7 2.6 %copy-start.1 = (bf16[128,2048]{1,0:T(8,128)(2,1)S(1)}, bf16[128,2048]{1,0:T(8,128)(2,1)}, u32[]{:S(2)}) copy-start(bf16[128,2048]{1,0:T(8,128)(2,1)} %get-tuple-element.27.refs_3_) | copy-start | bytes 1572868 | tf_op jit(solution)/shard_map/cond

commit v10 on v9

--- a/solution.py
+++ b/solution.py
@@ -193,8 +193,8 @@
 
     def tiles(first):
         query, grads = head.piece(0, first, step), head.piece(3, first, step)
-        for start in range(0, first, step):
-            head.tile(query, grads, first, start, step)
+        if first > 0:
+            head.tile(query, grads, first, 0, first)
         head.tile(query[rows:], grads[rows:], first + rows, first, rows)
 
     def sums(first):

time: 65 us -> 65 us (level)
  no operation moved by 1% of the time
where the time goes in v10:
time: 65 us; the launch traced here: 64.8 us
  blocking collectives  49.2 us (76%)
  Pallas kernels  11.7 us (18%)
  local copies, waits for them, and re-layouts  2.79 us (4%)
  between operations  0.82 us (1%)
    all_to_all x2, blocking collectives, exchange(): return lax.all_to_all(chunks, 'ctx', 0, 0, tiled=True)  49.2 us
    pallas_call x3, Pallas kernels, run(): pl.pallas_call(kernel, out_shape=out_shape, in_specs=in_specs, out_specs=...  11.7 us
    cond x8, local copies, waits for them, and re-layouts  2.78 us

profile of v10, /device:TPU:0, one launch (start us, length us, event | category | flops | bytes accessed | tf_op | source)
XLA Modules:
  0.0 64.8 jit_solution(10274407960474671218)
XLA Ops:
  0.6 64.0 %conditional.1 = ((bf16[128,2048]{1,0:T(8,128)(2,1)}, bf16[128,2048]{1,0:T(8,128)(2,1)}, bf16[128,2048]{1,0:T(8,128)(2,1)})) conditional(s32[]{:T(128)} %convert_element_type.3, (bf16[128,2048]{1,0:T(8,128)(2,1)}, bf16[128,2048]{1,0:T(8,128)(2,1)}, bf16[128,2048]{1,0:T(8,128)(2,1)}, bf16[128,2048]{1,0:T(8,128)(2,1)}, bf16[128,2048]{1,0:T(8,128)(2,1)}, ...), branch_computations={%region_0.1_spmd, %region_1.2_spmd} | conditional | bytes 15859776 | solution.py:328
  0.7 0.0 copy-start
  0.7 0.0 copy-start.1
  0.7 1.2 %fusion.3 = bf16[16,520,128]{2,1,0:T(8,128)(2,1)S(1)} fusion(bf16[128,2048]{1,0:T(8,128)(2,1)} %get-tuple-element.24.refs_0_), kind=kLoop, calls=%fused_computation.7 | loop fusion | bytes 1048576 | tf_op jit(solution)/shard_map/cond
  1.9 1.2 %fusion.2 = bf16[16,520,128]{2,1,0:T(8,128)(2,1)S(1)} fusion(bf16[16,520,128]{2,1,0:T(8,128)(2,1)S(1)} %fusion.3, bf16[128,2048]{1,0:T(8,128)(2,1)} %get-tuple-element.25.refs_1_), kind=kLoop, calls=%fused_computation.5 | loop fusion | bytes 1048576 | tf_op jit(solution)/shard_map/cond
  3.1 0.0 copy-done
  3.1 0.2 fusion.1
  3.3 0.0 copy-done.1
  3.3 0.2 fusion
  3.5 5.6 %near.1 = (f32[128,2048]{1,0:T(8,128)S(1)}, f32[128,2048]{1,0:T(8,128)S(1)}, f32[128,2048]{1,0:T(8,128)S(1)}, bf16[16,8,128]{2,1,0:T(8,128)(2,1)S(1)}) custom-call(bf16[128,2048]{1,0:T(8,128)(2,1)} %get-tuple-element.24.refs_0_, bf16[128,2048]{1,0:T(8,128)(2,1)} %get-tuple-element.25.refs_1_, bf16[128,2048]{1,0:T(8,128)(2,1)} %get-tuple-element.26.refs_2_, ...), custom_call_target="tpu_custom_call" | custom-call | tf_op jit(solution)/shard_map/cond/branch_0_fun/near/pallas_call | solution.py:270
  9.1 30.3 %all_to_all.16.refs_0_ = bf16[16,65,8,128]{3,2,1,0:T(8,128)(2,1)S(1)} all-to-all(bf16[16,65,8,128]{3,2,1,0:T(8,128)(2,1)S(1)} %bitcast.45), channel_id=1, replica_groups=mesh['ctx'=16,'doc'=8] {'ctx'}, dimensions={0} | all-to-all | bytes 4259840 | tf_op jit(solution)/shard_map/cond/branch_0_fun/exchange/all_to_all | solution.py:284
  39.4 4.8 %head_grads.2 = bf16[16,384,128]{2,1,0:T(8,128)(2,1)S(1)} custom-call(bf16[16,65,8,128]{3,2,1,0:T(8,128)(2,1)S(1)} %all_to_all.16.refs_0_), custom_call_target="tpu_custom_call" | custom-call | tf_op jit(solution)/shard_map/cond/branch_0_fun/head_grads/pallas_call | solution.py:270
  44.3 18.9 %all_to_all.17.recv_ref = bf16[16,384,128]{2,1,0:T(8,128)(2,1)S(1)} all-to-all(bf16[16,384,128]{2,1,0:T(8,128)(2,1)S(1)} %head_grads.2), channel_id=1, replica_groups=mesh['ctx'=16,'doc'=8] {'ctx'}, dimensions={0} | all-to-all | bytes 3145728 | tf_op jit(solution)/shard_map/cond/branch_0_fun/exchange/all_to_all | solution.py:284
  63.1 1.2 %unpack.2 = (bf16[128,2048]{1,0:T(8,128)(2,1)}, bf16[128,2048]{1,0:T(8,128)(2,1)}, bf16[128,2048]{1,0:T(8,128)(2,1)}) custom-call(bf16[16,384,128]{2,1,0:T(8,128)(2,1)S(1)} %all_to_all.17.recv_ref, f32[128,2048]{1,0:T(8,128)S(1)} %get-tuple-element.31.refs_0_, f32[128,2048]{1,0:T(8,128)S(1)} %get-tuple-element.32.refs_1_, ...), custom_call_target="tpu_custom_call" | custom-call | tf_op jit(solution)/shard_map/cond/branch_0_fun/unpack/pallas_call | solution.py:270
  (1 shorter events, 0.0 us)
Async XLA Ops:
  0.7 2.5 %copy-start = (bf16[128,2048]{1,0:T(8,128)(2,1)S(1)}, bf16[128,2048]{1,0:T(8,128)(2,1)}, u32[]{:S(2)}) copy-start(bf16[128,2048]{1,0:T(8,128)(2,1)} %get-tuple-element.26.refs_2_) | copy-start | bytes 1572868 | tf_op jit(solution)/shard_map/cond
  0.7 2.6 %copy-start.1 = (bf16[128,2048]{1,0:T(8,128)(2,1)S(1)}, bf16[128,2048]{1,0:T(8,128)(2,1)}, u32[]{:S(2)}) copy-start(bf16[128,2048]{1,0:T(8,128)(2,1)} %get-tuple-element.27.refs_3_) | copy-start | bytes 1572868 | tf_op jit(solution)/shard_map/cond
